TPU v7x, 32 devices: a whole 2x2x4 slice. The times are simulated.
32 devices in a mesh: groups: 2 (over y), row: 4 (over z), col: 4 (over x, core).
Axes of the slice: x: 2, y: 2, z: 4, core: 2. Of those that a mesh axis runs over, the one named last changes fastest.
Arguments:
- inputs: bfloat16 [1024, 8192], P(('groups', 'row'), 'col'), parts along dimension 0, may hold values from -6 to 6
- cotangent: bfloat16 [1024, 8192], P(('groups', 'row'), 'col'), parts along dimension 0, may hold values from -6 to 6
- w_gate: bfloat16 [8192, 14336], P('col', 'row'), may hold values from -0.0625 to 0.0625
- w_up: bfloat16 [8192, 14336], P('col', 'row'), may hold values from -0.0625 to 0.0625
- w_down: bfloat16 [14336, 8192], P('row', 'col'), may hold values from -0.046875 to 0.046875
Outputs:
- output: bfloat16 [1024, 8192], P(('groups', 'row'), 'col'), parts along dimension 0
- d_inputs: bfloat16 [1024, 8192], P(('groups', 'row'), 'col'), parts along dimension 0
- grad_gate: bfloat16 [16384, 14336], P(('groups', 'col'), 'row'), parts along dimension 0
- grad_up: bfloat16 [16384, 14336], P(('groups', 'col'), 'row'), parts along dimension 0
- grad_down: bfloat16 [28672, 8192], P(('groups', 'row'), 'col'), parts along dimension 0
There are 2 independent parts, one for each index of `groups`. A program takes and returns all parts, laid end to end along the dimension named above; an argument that names none is the same for every part. Nothing has to cross between parts.
All inputs are finite; a program needn't handle non-finite values.
Results may differ from a plain program's by a relative error of at most 0.0051.
Values may be sent and summed in bfloat16 or wider, within the bound.
No kernel may reach another device: no remote copies, remote signals or barrier semaphores. Data moves between devices by JAX's collectives and lax.ppermute only.
A program may use at most 256 MiB of HBM per device.

v0:
```python
import jax
import jax.numpy as jnp
from jax import lax
from jax.sharding import PartitionSpec as P


def pointwise(gate_part, up_part, back_grad):
    logistic = jax.nn.sigmoid(gate_part)
    swish = gate_part * logistic
    hidden = (swish * up_part).astype(jnp.bfloat16)
    d_up = (back_grad * swish).astype(jnp.bfloat16)
    d_gate = (back_grad * up_part * logistic * (1.0 + gate_part * (1.0 - logistic))).astype(
        jnp.bfloat16
    )
    return (hidden, d_gate, d_up)


def local(inputs, cotangent, w_gate, w_up, w_down):
    full_inputs, full_cotangent = (
        lax.all_gather(inputs, "row", axis=0, tiled=True),
        lax.all_gather(cotangent, "row", axis=0, tiled=True),
    )
    hidden_width = w_gate.shape[1]
    feature_width = w_down.shape[1]
    contract_last = (((1,), (1,)), ((), ()))
    contract_rows = (((0,), (0,)), ((), ()))
    gate_part = jnp.dot(full_inputs, w_gate, preferred_element_type=jnp.float32)
    up_part = jnp.dot(full_inputs, w_up, preferred_element_type=jnp.float32)
    back_grad = lax.dot_general(
        full_cotangent, w_down, contract_last, preferred_element_type=jnp.float32
    )
    shares = lax.psum_scatter(
        jnp.concatenate([gate_part, up_part, back_grad], axis=1),
        "col",
        scatter_dimension=0,
        tiled=True,
    )
    hidden_share, gate_share, up_share = pointwise(
        shares[:, :hidden_width],
        shares[:, hidden_width : 2 * hidden_width],
        shares[:, 2 * hidden_width :],
    )
    hidden, d_gate, d_up = (
        lax.all_gather(hidden_share, "col", axis=0, tiled=True),
        lax.all_gather(gate_share, "col", axis=0, tiled=True),
        lax.all_gather(up_share, "col", axis=0, tiled=True),
    )
    grad_down = lax.dot_general(
        hidden, full_cotangent, contract_rows, preferred_element_type=jnp.float32
    ).astype(jnp.bfloat16)
    grad_gate = lax.dot_general(
        full_inputs, d_gate, contract_rows, preferred_element_type=jnp.float32
    ).astype(jnp.bfloat16)
    grad_up = lax.dot_general(
        full_inputs, d_up, contract_rows, preferred_element_type=jnp.float32
    ).astype(jnp.bfloat16)
    forward_term = jnp.dot(hidden, w_down, preferred_element_type=jnp.float32)
    back_term = lax.dot_general(d_gate, w_gate, contract_last, preferred_element_type=jnp.float32)
    back_term = back_term + lax.dot_general(
        d_up, w_up, contract_last, preferred_element_type=jnp.float32
    )
    results = lax.psum_scatter(
        jnp.concatenate([forward_term, back_term], axis=1), "row", scatter_dimension=0, tiled=True
    )
    output = results[:, :feature_width].astype(jnp.bfloat16)
    d_inputs = results[:, feature_width:].astype(jnp.bfloat16)
    return (output, d_inputs, grad_gate, grad_up, grad_down)


def solution(mesh):
    return jax.shard_map(
        local,
        mesh=mesh,
        in_specs=(
            P(("groups", "row"), "col"),
            P(("groups", "row"), "col"),
            P("col", "row"),
            P("col", "row"),
            P("row", "col"),
        ),
        out_specs=(
            P(("groups", "row"), "col"),
            P(("groups", "row"), "col"),
            P(("groups", "col"), "row"),
            P(("groups", "col"), "row"),
            P(("groups", "row"), "col"),
        ),
        check_vma=False,
    )
```

profile of v0, /device:TPU:0, one launch (start us, length us, event | category | flops | bytes accessed | tf_op | source)
XLA Modules:
  0.0 562.5 jit_solution(2884977529978058369)
XLA Ops:
  7.2 0.0 all-gather.6.cloned.1.call-start
  7.2 0.7 all-gather.6.cloned.1.call-update
  7.9 0.0 all-gather.8.cloned.1.call-start
  7.9 0.7 all-gather.8.cloned.1.call-update
  8.6 0.0 reduce-scatter.3.cloned.1.call-start
  8.7 49.5 %all-gather.6.cloned.1.call-done = bf16[512,2048]{1,0:T(8,128)(2,1)} async-done(((bf16[128,2048]{1,0:T(8,128)(2,1)}), bf16[512,2048]{1,0:T(8,128)(2,1)}) %all-gather.6.cloned.1.call-update) | async-done | bytes 2097168 | tf_op jit(solution)/shard_map/all_gather | solution.py:20
  58.2 0.0 copy-start.3
  58.2 15.5 %fusion.4 = f32[512,3584]{1,0:T(8,128)} fusion(bf16[512,2048]{1,0:T(8,128)(2,1)} %all-gather.6.cloned.1.call-done, bf16[2048,3584]{1,0:T(8,128)(2,1)} %param.7), kind=kOutput, calls=%fused_computation.14 | convolution fusion | flops 7516192768 | bytes 24117248 | tf_op jit(solution)/shard_map/dot_general | solution.py:27
  73.7 0.0 copy-done.3
  73.7 12.9 %fusion.5 = f32[512,3584]{1,0:T(8,128)} fusion(bf16[512,2048]{1,0:T(8,128)(2,1)S(1)} %copy-done.3, bf16[2048,3584]{1,0:T(8,128)(2,1)} %param.8), kind=kOutput, calls=%fused_computation.15 | convolution fusion | flops 7516192768 | bytes 24117248 | tf_op jit(solution)/shard_map/dot_general | solution.py:28
  86.6 17.9 %all-gather.8.cloned.1.call-done = bf16[512,2048]{1,0:T(8,128)(2,1)} async-done(((bf16[128,2048]{1,0:T(8,128)(2,1)}), bf16[512,2048]{1,0:T(8,128)(2,1)}) %all-gather.8.cloned.1.call-update) | async-done | bytes 2097168 | tf_op jit(solution)/shard_map/all_gather | solution.py:21
  104.5 0.0 copy-start
  104.5 0.0 copy-start.1
  104.5 13.7 %fusion.6 = f32[512,3584]{1,0:T(8,128)} fusion(bf16[512,2048]{1,0:T(8,128)(2,1)} %all-gather.8.cloned.1.call-done, bf16[3584,2048]{1,0:T(8,128)(2,1)} %param.9), kind=kOutput, calls=%fused_computation.16 | convolution fusion | flops 7516192768 | bytes 24117248 | tf_op jit(solution)/shard_map/dot_general | solution.py:29
  118.2 0.0 copy-done
  118.2 0.0 copy-done.1
  118.2 10.4 %pad_maximum_fusion = f32[512,10752]{1,0:T(8,128)} fusion(f32[512,3584]{1,0:T(8,128)} %fusion.6, f32[512,3584]{1,0:T(8,128)S(1)} %copy-done.1, f32[512,3584]{1,0:T(8,128)S(1)} %copy-done), kind=kLoop, calls=%fused_computation | loop fusion | flops 11010048 | bytes 44040192 | tf_op jit(solution)/shard_map/concatenate | solution.py:33
  128.6 0.0 reduce-scatter.3.cloned.1.call-update
  128.6 0.0 all-gather.12.cloned.1.call-start
  128.7 158.7 %reduce-scatter.3.cloned.1.call-done = f32[128,10752]{1,0:T(8,128)} async-done(((f32[512,10752]{1,0:T(8,128)}), f32[128,10752]{1,0:T(8,128)}) %reduce-scatter.3.cloned.1.call-update) | async-done | bytes 5505040 | tf_op jit(solution)/shard_map/reduce_scatter | solution.py:32
  287.4 5.2 multiply_convert_fusion.2
  292.6 0.0 all-gather.12.cloned.1.call-update
  292.6 0.0 all-gather.10.cloned.1.call-start
  292.7 0.5 all-gather.10.cloned.1.call-update
  293.2 0.0 all-gather.14.cloned.1.call-start
  293.3 0.5 all-gather.14.cloned.1.call-update
  293.8 0.2 reduce-scatter.5.cloned.1.call-start
  294.0 30.3 %all-gather.12.cloned.1.call-done = bf16[512,3584]{1,0:T(8,128)(2,1)} async-done(((bf16[128,3584]{1,0:T(8,128)(2,1)}), bf16[512,3584]{1,0:T(8,128)(2,1)}) %all-gather.12.cloned.1.call-update) | async-done | bytes 3670032 | tf_op jit(solution)/shard_map/all_gather | solution.py:45
  324.3 13.4 %fusion.8 = f32[512,2048]{1,0:T(8,128)} fusion(bf16[512,3584]{1,0:T(8,128)(2,1)} %all-gather.12.cloned.1.call-done, bf16[2048,3584]{1,0:T(8,128)(2,1)} %param.7), kind=kOutput, calls=%fused_computation.18 | convolution fusion | flops 7516192768 | bytes 22544384 | tf_op jit(solution)/shard_map/dot_general | solution.py:58
  337.7 20.2 %all-gather.10.cloned.1.call-done = bf16[512,3584]{1,0:T(8,128)(2,1)} async-done(((bf16[128,3584]{1,0:T(8,128)(2,1)}), bf16[512,3584]{1,0:T(8,128)(2,1)}) %all-gather.10.cloned.1.call-update) | async-done | bytes 3670032 | tf_op jit(solution)/shard_map/all_gather | solution.py:44
  357.9 13.4 %fusion.7 = f32[512,2048]{1,0:T(8,128)} fusion(bf16[512,3584]{1,0:T(8,128)(2,1)} %all-gather.10.cloned.1.call-done, bf16[3584,2048]{1,0:T(8,128)(2,1)} %param.9), kind=kOutput, calls=%fused_computation.17 | convolution fusion | flops 7516192768 | bytes 22544384 | tf_op jit(solution)/shard_map/dot_general | solution.py:57
  371.3 20.3 %all-gather.14.cloned.1.call-done = bf16[512,3584]{1,0:T(8,128)(2,1)} async-done(((bf16[128,3584]{1,0:T(8,128)(2,1)}), bf16[512,3584]{1,0:T(8,128)(2,1)}) %all-gather.14.cloned.1.call-update) | async-done | bytes 3670032 | tf_op jit(solution)/shard_map/all_gather | solution.py:46
  391.5 0.0 copy-start.2
  391.6 12.9 %convolution_add_fusion = f32[512,2048]{1,0:T(8,128)S(1)} fusion(f32[512,2048]{1,0:T(8,128)} %fusion.8, bf16[512,3584]{1,0:T(8,128)(2,1)} %all-gather.14.cloned.1.call-done, bf16[2048,3584]{1,0:T(8,128)(2,1)} %param.8), kind=kOutput, calls=%fused_computation.7 | convolution fusion | flops 7517241344 | bytes 26738688 | tf_op jit(solution)/shard_map/dot_general | solution.py:59
  404.4 0.0 copy-done.2
  404.4 3.8 pad_maximum_fusion.1
  408.2 0.0 reduce-scatter.5.cloned.1.call-update
  408.3 13.2 %fusion = bf16[2048,3584]{0,1:T(8,128)(2,1)} fusion(bf16[512,3584]{1,0:T(8,128)(2,1)} %all-gather.12.cloned.1.call-done, bf16[512,2048]{1,0:T(8,128)(2,1)S(1)} %copy-done.3), kind=kOutput, calls=%fused_computation.4 | convolution fusion | flops 7523532800 | bytes 20447232 | tf_op jit(solution)/shard_map/dot_general | solution.py:51
  421.5 18.7 %copy.10 = bf16[2048,3584]{1,0:T(8,128)(2,1)} copy(bf16[2048,3584]{0,1:T(8,128)(2,1)} %fusion) | data formatting | bytes 29360128
  440.2 13.2 %fusion.1 = bf16[2048,3584]{0,1:T(8,128)(2,1)} fusion(bf16[512,3584]{1,0:T(8,128)(2,1)} %all-gather.14.cloned.1.call-done, bf16[512,2048]{1,0:T(8,128)(2,1)S(1)} %copy-done.3), kind=kOutput, calls=%fused_computation.5 | convolution fusion | flops 7523532800 | bytes 20447232 | tf_op jit(solution)/shard_map/dot_general | solution.py:54
  453.3 0.0 copy-start.4
  453.3 18.9 %copy.11 = bf16[2048,3584]{1,0:T(8,128)(2,1)} copy(bf16[2048,3584]{0,1:T(8,128)(2,1)} %fusion.1) | data formatting | bytes 29360128
  472.2 0.0 copy-done.4
  472.2 13.2 %convolution_convert_fusion = bf16[3584,2048]{1,0:T(8,128)(2,1)} fusion(bf16[512,3584]{1,0:T(8,128)(2,1)} %all-gather.10.cloned.1.call-done, bf16[512,2048]{1,0:T(8,128)(2,1)S(1)} %copy-done.4), kind=kOutput, calls=%fused_computation.1 | convolution fusion | flops 7523532800 | bytes 20447232 | tf_op jit(solution)/shard_map/dot_general | solution.py:48
  485.4 67.5 %reduce-scatter.5.cloned.1.call-done = f32[128,4096]{1,0:T(8,128)} async-done(((f32[512,4096]{1,0:T(8,128)}), f32[128,4096]{1,0:T(8,128)}) %reduce-scatter.5.cloned.1.call-update) | async-done | bytes 2097168 | tf_op jit(solution)/shard_map/reduce_scatter | solution.py:62
  552.9 1.7 convert.4
  554.6 1.0 fusion.3
Async XLA Ops:
  7.2 51.1 %all-gather.6.cloned.1.call-start = ((), (), s32[]{:S(2)}) async-start(), calls=%async_computation.2 | async-start | bytes 2621440 | tf_op jit(solution)/shard_map/all_gather | solution.py:20
  7.9 96.6 %all-gather.8.cloned.1.call-start = ((), (), s32[]{:S(2)}) async-start(), calls=%async_computation.3 | async-start | bytes 2621440 | tf_op jit(solution)/shard_map/all_gather | solution.py:21
  8.6 278.8 %reduce-scatter.3.cloned.1.call-start = ((), (), s32[]{:S(2)}) async-start(), calls=%async_computation.4 | async-start | bytes 27525120 | tf_op jit(solution)/shard_map/reduce_scatter | solution.py:32
  58.2 15.5 %copy-start.3 = (bf16[512,2048]{1,0:T(8,128)(2,1)S(1)}, bf16[512,2048]{1,0:T(8,128)(2,1)}, u32[]{:S(2)}) copy-start(bf16[512,2048]{1,0:T(8,128)(2,1)} %all-gather.6.cloned.1.call-done) | copy-start | bytes 6291460
  104.5 13.7 %copy-start = (f32[512,3584]{1,0:T(8,128)S(1)}, f32[512,3584]{1,0:T(8,128)}, u32[]{:S(2)}) copy-start(f32[512,3584]{1,0:T(8,128)} %fusion.4) | copy-start | bytes 22020100
  104.5 13.7 %copy-start.1 = (f32[512,3584]{1,0:T(8,128)S(1)}, f32[512,3584]{1,0:T(8,128)}, u32[]{:S(2)}) copy-start(f32[512,3584]{1,0:T(8,128)} %fusion.5) | copy-start | bytes 22020100
  128.6 195.7 %all-gather.12.cloned.1.call-start = ((), (), s32[]{:S(2)}) async-start(), calls=%async_computation.6 | async-start | bytes 4587520 | tf_op jit(solution)/shard_map/all_gather | solution.py:45
  292.6 65.3 %all-gather.10.cloned.1.call-start = ((), (), s32[]{:S(2)}) async-start(), calls=%async_computation.5 | async-start | bytes 4587520 | tf_op jit(solution)/shard_map/all_gather | solution.py:44
  293.2 98.3 %all-gather.14.cloned.1.call-start = ((), (), s32[]{:S(2)}) async-start(), calls=%async_computation.7 | async-start | bytes 4587520 | tf_op jit(solution)/shard_map/all_gather | solution.py:46
  293.8 259.1 %reduce-scatter.5.cloned.1.call-start = ((), (), s32[]{:S(2)}) async-start(), calls=%async_computation.8 | async-start | bytes 10485760 | tf_op jit(solution)/shard_map/reduce_scatter | solution.py:62
  391.5 12.9 %copy-start.2 = (f32[512,2048]{1,0:T(8,128)S(1)}, f32[512,2048]{1,0:T(8,128)}, u32[]{:S(2)}) copy-start(f32[512,2048]{1,0:T(8,128)} %fusion.7) | copy-start | bytes 12582916
  453.3 18.9 %copy-start.4 = (bf16[512,2048]{1,0:T(8,128)(2,1)S(1)}, bf16[512,2048]{1,0:T(8,128)(2,1)}, u32[]{:S(2)}) copy-start(bf16[512,2048]{1,0:T(8,128)(2,1)} %all-gather.8.cloned.1.call-done) | copy-start | bytes 6291460
Sparse Core Ops, SparseCore 0:
  9.6 48.6 all-gather.5
  59.8 44.6 all-gather.7
  128.8 158.6 reduce-scatter.2
  292.8 31.5 all-gather.11
  326.4 31.4 all-gather.9
  360.0 31.5 all-gather.13
  408.4 144.4 reduce-scatter.4
where the time goes:
time: 564 us; the launch traced here: 562 us
  waiting for transfers between devices  367 us (65%)
  matrix products  121 us (21%)
  local copies, waits for them, and re-layouts  38.6 us (7%)
  other arithmetic  21.1 us (4%)
  between operations  14.2 us (3%)
    reduce_scatter x1, waiting for transfers between devices, local(): lax.psum_scatter(jnp.concatenate([gate_part, up_part, back_grad], axis=1)...  159 us
    reduce_scatter x1, waiting for transfers between devices, local(): lax.psum_scatter(jnp.concatenate([forward_term, back_term], axis=1), 'row...  67.5 us
    all_gather x1, waiting for transfers between devices, local(): lax.all_gather(inputs, 'row', axis=0, tiled=True)  49.5 us
    unnamed x12, local copies, waits for them, and re-layouts  37.6 us
    all_gather x1, waiting for transfers between devices, local(): lax.all_gather(gate_share, 'col', axis=0, tiled=True)  30.3 us
    all_gather x1, waiting for transfers between devices, local(): lax.all_gather(up_share, 'col', axis=0, tiled=True)  20.3 us
    all_gather x1, waiting for transfers between devices, local(): lax.all_gather(hidden_share, 'col', axis=0, tiled=True)  20.2 us
    all_gather x1, waiting for transfers between devices, local(): lax.all_gather(cotangent, 'row', axis=0, tiled=True)  17.9 us
  transfers between devices with their start and end apart: 7, of which 7 were waited for; matrix products, arithmetic and copies ran while one was open for 24% of the time, Pallas kernels for 0%

commit v1 on v0

v1 whole, which is shorter than its diff:
```python
import jax
import jax.numpy as jnp
from jax import lax
from jax.experimental import pallas as pl
from jax.experimental.pallas import tpu as pltpu
from jax.sharding import PartitionSpec as P

BF16 = jnp.bfloat16
F32 = jnp.float32
NT = (((1,), (1,)), ((), ()))
TN = (((0,), (0,)), ((), ()))
PARAMS = pltpu.CompilerParams(vmem_limit_bytes=66_900_000)
T = 256


def pointwise(gate_part, up_part, back_grad):
    logistic = jax.nn.sigmoid(gate_part)
    swish = gate_part * logistic
    hidden = (swish * up_part).astype(BF16)
    d_up = (back_grad * swish).astype(BF16)
    d_gate = (back_grad * up_part * logistic * (1.0 + gate_part * (1.0 - logistic))).astype(BF16)
    return (hidden, d_gate, d_up)


VMEM = pl.BlockSpec(memory_space=pltpu.VMEM)
SMEM = pl.BlockSpec(memory_space=pltpu.SMEM)
ANY = pl.BlockSpec(memory_space=pltpu.HBM)
DEEP = pl.Buffered(4)


def tile_of(core, tiles, t0, n):
    def tile(j):
        return jnp.where(j < n, (1 - core) * tiles + t0 + j, core * tiles + t0 + j - n)

    return tile


def weight_specs(tile, F, mode):
    return [
        pl.BlockSpec((F, T), lambda j: (0, tile(j)), pipeline_mode=mode),
        pl.BlockSpec((F, T), lambda j: (0, tile(j)), pipeline_mode=mode),
        pl.BlockSpec((T, F), lambda j: (tile(j), 0), pipeline_mode=mode),
    ]


def chain_call(
    name, body, after, args, in_specs, out_shape, out_specs, scratch=(), grid=(), aliases=None
):
    kernel = body
    if after is not None:
        args = list(args) + [after]
        in_specs = list(in_specs) + [ANY]
        count = len(args)

        def kernel(*refs):
            return body(*refs[: count - 1], *refs[count:])

    return pl.pallas_call(
        kernel,
        name=name,
        out_shape=out_shape,
        in_specs=in_specs,
        out_specs=out_specs,
        scratch_shapes=list(scratch),
        grid=grid,
        input_output_aliases=aliases or {},
        compiler_params=PARAMS,
        cost_estimate=pl.CostEstimate(flops=1, bytes_accessed=1, transcendentals=0),
    )(*args)


def forward_call(core, weights, rows, after):
    M, F = rows[0][0].shape[-2:]
    R = M * len(rows)
    n = weights[0].shape[1] // T // 2
    held = [v for some in rows for v in some]

    def body(s, *refs):
        wg_hbm, wu_hbm, wd_hbm, *outs = refs[len(held) : -2]
        x_and_c, sem = refs[-2:]
        tile = tile_of(s[0], n, 0, n)
        copies = []
        at = 0
        for k, some in enumerate(rows):
            for i in range(2):
                source = refs[at + i] if len(some) == 2 else refs[at].at[i]
                copies.append(
                    pltpu.make_async_copy(
                        source, x_and_c.at[i, pl.ds(k * M, M)], sem.at[len(copies)]
                    )
                )
            at += len(some)
        for copy in copies:
            copy.start()
        for copy in copies:
            copy.wait()

        def step(wg, wu, wd, sent_gate, sent_up, sent_back, kept):
            j = pl.program_id(0)

            def sums():
                yield jnp.dot(x_and_c[0], wg[...], preferred_element_type=F32)
                yield jnp.dot(x_and_c[0], wu[...], preferred_element_type=F32)
                yield lax.dot_general(x_and_c[1], wd[...], NT, preferred_element_type=F32)

            @pl.when(j < n)
            def _():
                for out, value in zip((sent_gate, sent_up, sent_back), sums()):
                    out[...] = value.astype(BF16)

            @pl.when(j >= n)
            def _():
                for k, value in enumerate(sums()):
                    kept[k] = value

        pltpu.emit_pipeline(
            step,
            grid=(2 * n,),
            in_specs=weight_specs(tile, F, DEEP),
            out_specs=[pl.BlockSpec((R, T), lambda j: (0, jnp.minimum(j, n - 1)))] * 3
            + [pl.BlockSpec((3, R, T), lambda j: (0, 0, jnp.maximum(j - n, 0)))],
        )(wg_hbm, wu_hbm, wd_hbm, *outs)

    return chain_call(
        "sums",
        body,
        after,
        [core, *held, *weights],
        [SMEM] + [ANY] * (len(held) + 3),
        [jax.ShapeDtypeStruct((R, n * T), BF16)] * 3
        + [jax.ShapeDtypeStruct((3, R, n * T), F32)],
        [ANY] * 4,
        [pltpu.VMEM((2, R, F), BF16), pltpu.SemaphoreType.DMA((2 * len(rows),))],
    )


def hold_call(array, after):
    def body(array_ref, out_ref):
        del array_ref, out_ref

    return chain_call(
        "hold",
        body,
        after,
        [array],
        [ANY],
        jax.ShapeDtypeStruct(array.shape, array.dtype),
        ANY,
        aliases={0: 0},
    )


def half_specs(M, width, k):
    three = pl.BlockSpec((3, M, width // 2), lambda j: (0, k, j))
    one = pl.BlockSpec((M, width // 2), lambda j: (k, j))
    return three, one


def add_call(kept, came, k, M, after):
    width = kept.shape[2]
    three, one = half_specs(M, width, k)

    def body(kept_ref, gate, up, back, send):
        for i, ref in enumerate((gate, up, back)):
            send[i] = (kept_ref[i] + ref[...].astype(F32)).astype(BF16)

    return chain_call(
        "share",
        body,
        after,
        [kept, *came],
        [three, one, one, one],
        jax.ShapeDtypeStruct((3, M, width), BF16),
        half_specs(M, width, 0)[0],
        grid=(2,),
    )


def pointwise_call(kept, came, k, chip, after):
    _, M, width = chip.shape
    three, one = half_specs(M, width, k)
    three_out, one_out = half_specs(M, width, 0)

    def body(kept_ref, gate, up, back, chip_ref, *outs):
        for at in range(0, width // 2, 128):
            cut = slice(at, at + 128)
            sums = [
                kept_ref[i, :, cut] + ref[:, cut].astype(F32) + chip_ref[i, :, cut].astype(F32)
                for i, ref in enumerate((gate, up, back))
            ]
            for out, value in zip(outs, pointwise(*sums)):
                out[:, cut] = value

    return chain_call(
        "point",
        body,
        after,
        [kept, *came, chip],
        [three, one, one, one, three_out],
        [jax.ShapeDtypeStruct((M, width), BF16)] * 3,
        [one_out] * 3,
        grid=(2,),
    )


def results_specs(hs, t0, n, mode):
    specs = []
    for h in hs:
        m = h[0].shape[0]
        specs += [pl.BlockSpec((m, T), lambda j: (0, t0 + jnp.minimum(j, n - 1)), pipeline_mode=mode)] * 3
        specs += [pl.BlockSpec((m, T), lambda j: (0, t0 + jnp.maximum(j - n, 0)), pipeline_mode=mode)] * 3
    return specs


def each_half(n, refs, work):
    j = pl.program_id(0)

    def rows(lo):
        return [
            jnp.concatenate([refs[at + lo + k][...] for at in range(0, len(refs), 6)], axis=0)
            for k in range(3)
        ]

    @pl.when(j < n)
    def _():
        work(*rows(0))

    @pl.when(j >= n)
    def _():
        work(*rows(3))


def backward_call(core, weights, span, hs, dtypes, after):
    t0, n = span
    F = weights[0].shape[0]
    tiles = weights[0].shape[1] // T // 2
    M = hs[0][0].shape[0]
    R = M * len(hs)

    def body(s, wg_hbm, wu_hbm, wd_hbm, *refs):
        h_hbm = refs[: 6 * len(hs)]
        *outs, acc = refs[6 * len(hs) :]
        tile = tile_of(s[0], tiles, t0, n)
        acc[...] = jnp.zeros_like(acc)

        def step(wg, wu, wd, *h):
            def work(hid, dg, du):
                acc[0] += jnp.dot(hid, wd[...], preferred_element_type=F32)
                acc[1] += lax.dot_general(
                    dg, wg[...], NT, preferred_element_type=F32
                ) + lax.dot_general(du, wu[...], NT, preferred_element_type=F32)

            each_half(n, h, work)

        pltpu.emit_pipeline(
            step,
            grid=(2 * n,),
            in_specs=weight_specs(tile, F, DEEP) + results_specs(hs, t0, n, DEEP),
        )(wg_hbm, wu_hbm, wd_hbm, *h_hbm)
        for k, out in enumerate(outs):
            out[...] = acc[:, k * M : (k + 1) * M].astype(out.dtype)

    flat = [v for h in hs for v in h]
    return chain_call(
        "back",
        body,
        after,
        [core, *weights, *flat],
        [SMEM] + [ANY] * (3 + len(flat)),
        [jax.ShapeDtypeStruct((2, M, F), dtype) for dtype in dtypes],
        [VMEM] * len(hs),
        [pltpu.VMEM((2, R, F), F32)],
    )


def join_call(part, came, split, after):
    _, M, F = part.shape
    both = pl.BlockSpec((2, M // 2, F), lambda j: (0, j, 0))

    def body(part_ref, came_ref, *outs):
        for i in range(2):
            value = (part_ref[i] + came_ref[i].astype(F32)).astype(BF16)
            if split:
                outs[i][...] = value
            else:
                outs[0][i] = value

    if split:
        shapes, specs = [(M, F)] * 2, [pl.BlockSpec((M // 2, F), lambda j: (j, 0))] * 2
    else:
        shapes, specs = [(2, M, F)], [both]
    return chain_call(
        "join",
        body,
        after,
        [part, came],
        [both, both],
        [jax.ShapeDtypeStruct(shape, BF16) for shape in shapes],
        specs,
        grid=(2,),
    )


def grads_call(core, span, rows, hs, shapes, after):
    t0, n = span
    R = len(rows)
    M, F = rows[0][0].shape[-2:]
    held = [v for some in rows for v in some]
    tiles = shapes[0][1] // T // 2

    def body(s, *refs):
        h_hbm = refs[len(held) : len(held) + 6 * R]
        gate_hbm, up_hbm, down_hbm, x_rows, c_rows, x_in, sem = refs[len(held) + 6 * R :]
        tile = tile_of(s[0], tiles, t0, n)
        copies = []
        at = 0
        for k, some in enumerate(rows):
            x, c = (refs[at], refs[at + 1]) if len(some) == 2 else (refs[at].at[0], refs[at].at[1])
            at += len(some)
            copies.append(pltpu.make_async_copy(x, x_in.at[k], sem.at[k]))
            copies.append(pltpu.make_async_copy(c, c_rows.at[pl.ds(k * M, M)], sem.at[R + k]))
        for copy in copies[::2] + copies[1::2]:
            copy.start()
        for k in range(R):
            copies[2 * k].wait()
            x_rows[:, k * M : (k + 1) * M] = x_in[k].T
        for copy in copies[1::2]:
            copy.wait()

        def step(*h):
            h, (gate, up, down) = h[:-3], h[-3:]

            def work(hid, dg, du):
                gate[...] = jnp.dot(x_rows[...], dg, preferred_element_type=F32).astype(BF16)
                up[...] = jnp.dot(x_rows[...], du, preferred_element_type=F32).astype(BF16)
                down[...] = lax.dot_general(
                    hid, c_rows[...], TN, preferred_element_type=F32
                ).astype(BF16)

            each_half(n, h, work)

        pltpu.emit_pipeline(
            step,
            grid=(2 * n,),
            in_specs=results_specs(hs, t0, n, None),
            out_specs=weight_specs(tile, F, None),
        )(*h_hbm, gate_hbm, up_hbm, down_hbm)

    flat = [v for h in hs for v in h]
    return chain_call(
        "grads",
        body,
        after,
        [core, *held, *flat],
        [SMEM] + [ANY] * (len(held) + len(flat)),
        [jax.ShapeDtypeStruct(s, BF16) for s in shapes],
        [ANY] * 3,
        [
            pltpu.VMEM((F, R * M), BF16),
            pltpu.VMEM((R * M, F), BF16),
            pltpu.VMEM((R, M, F), BF16),
            pltpu.SemaphoreType.DMA((2 * R,)),
        ],
    )


ORDER = ["S0", "A0", "W1", "S1", "W2", "A1", "S2", "P0", "A2", "S3", "P1", "A3", "B01", "P2", "B2"]
ORDER += ["J2", "P3", "B3", "J3", "G", "J0"]


def tiled(rows, cols):
    def local(inputs, cotangent, w_gate, w_up, w_down):
        weights = (w_gate, w_up, w_down)
        shapes = [w.shape for w in weights]
        full = (0, w_gate.shape[1] // T // 2)
        core = (lax.axis_index("col") % 2).astype(jnp.int32).reshape(1)
        to_core = lambda v: lax.ppermute(v, "col", [(i, i ^ 1) for i in range(cols)])
        to_chip = lambda v: lax.ppermute(v, "col", [(i, i ^ 2) for i in range(cols)])
        onward = lambda v: lax.ppermute(v, "row", [(i, (i + 1) % rows) for i in range(rows)])
        last = [None]

        def then(call, *args):
            out = call(*args, last[0])
            last[0] = out[0] if isinstance(out, (list, tuple)) else out
            return out

        held = [(inputs, cotangent), (onward(jnp.stack([inputs, cotangent])),)]

        M = inputs.shape[0]
        kept, came, block, chip, h, totals = {}, {}, {}, {}, {}, {}
        for word in ORDER:
            step, digits = word[0], [int(d) for d in word[1:]]
            k = digits[0] if digits else None
            if step == "S":
                *sent, own = then(forward_call, core, weights, [held[k] for k in digits])
                sent = [to_core(v) for v in sent]
                for at, k in enumerate(digits):
                    kept[k], came[k], block[k] = own, sent, at
            elif step == "W":
                held[k] = (then(hold_call, held[k][0]),)
                held.append((onward(held[k][0]),))
            elif step == "A":
                chip[k] = to_chip(then(add_call, kept[k], came[k], block[k], M))
            elif step == "P":
                own = then(pointwise_call, kept[k], came[k], block[k], chip[k])
                h[k] = [to_core(v) for v in own] + list(own)
            elif step == "B":
                dtypes = [BF16 if k == 1 else F32 for k in digits]
                sums = then(backward_call, core, weights, full, [h[k] for k in digits], dtypes)
                totals.update(zip(digits, sums))
                if 1 in digits:
                    moving = onward(totals[1])
            elif step == "J" and k:
                moving = onward(*then(join_call, totals[k], moving, False))
            elif step == "J":
                output, d_inputs = then(join_call, totals[0], moving, True)
            elif step == "G":
                grads = then(grads_call, core, full, held, [h[k] for k in range(rows)], shapes)
        return (output, d_inputs, *grads)

    return local


def plain(inputs, cotangent, w_gate, w_up, w_down):
    full_inputs, full_cotangent = (
        lax.all_gather(inputs, "row", axis=0, tiled=True),
        lax.all_gather(cotangent, "row", axis=0, tiled=True),
    )
    hidden_width = w_gate.shape[1]
    feature_width = w_down.shape[1]
    gate_part = jnp.dot(full_inputs, w_gate, preferred_element_type=F32)
    up_part = jnp.dot(full_inputs, w_up, preferred_element_type=F32)
    back_grad = lax.dot_general(full_cotangent, w_down, NT, preferred_element_type=F32)
    shares = lax.psum_scatter(
        jnp.concatenate([gate_part, up_part, back_grad], axis=1),
        "col",
        scatter_dimension=0,
        tiled=True,
    )
    hidden, d_gate, d_up = (
        lax.all_gather(share, "col", axis=0, tiled=True)
        for share in pointwise(
            shares[:, :hidden_width],
            shares[:, hidden_width : 2 * hidden_width],
            shares[:, 2 * hidden_width :],
        )
    )
    grad_down = lax.dot_general(hidden, full_cotangent, TN, preferred_element_type=F32)
    grad_gate = lax.dot_general(full_inputs, d_gate, TN, preferred_element_type=F32)
    grad_up = lax.dot_general(full_inputs, d_up, TN, preferred_element_type=F32)
    forward_term = jnp.dot(hidden, w_down, preferred_element_type=F32)
    back_term = lax.dot_general(d_gate, w_gate, NT, preferred_element_type=F32)
    back_term = back_term + lax.dot_general(d_up, w_up, NT, preferred_element_type=F32)
    results = lax.psum_scatter(
        jnp.concatenate([forward_term, back_term], axis=1), "row", scatter_dimension=0, tiled=True
    )
    return (
        results[:, :feature_width].astype(BF16),
        results[:, feature_width:].astype(BF16),
        grad_gate.astype(BF16),
        grad_up.astype(BF16),
        grad_down.astype(BF16),
    )


def solution(mesh):
    rows, cols = mesh.shape["row"], mesh.shape["col"]

    def local(inputs, cotangent, w_gate, w_up, w_down):
        step = plain
        if rows == 4 and cols == 4 and w_gate.shape[1] % (14 * T) == 0 and inputs.shape[0] % 16 == 0:
            step = tiled(rows, cols)
        return step(inputs, cotangent, w_gate, w_up, w_down)

    return jax.shard_map(
        local,
        mesh=mesh,
        in_specs=(
            P(("groups", "row"), "col"),
            P(("groups", "row"), "col"),
            P("col", "row"),
            P("col", "row"),
            P("row", "col"),
        ),
        out_specs=(
            P(("groups", "row"), "col"),
            P(("groups", "row"), "col"),
            P(("groups", "col"), "row"),
            P(("groups", "col"), "row"),
            P(("groups", "row"), "col"),
        ),
        check_vma=False,
    )
```

time: 564 us -> 239 us (0.42)
  waiting for transfers between devices: 367 us -> 15.7 us
  Pallas kernels: 0 us -> 201 us
  matrix products: 121 us -> 0 us
  local copies, waits for them, and re-layouts: 38.6 us -> 0 us
  other arithmetic: 21.1 us -> 2.27 us
  starting transfers between devices: 0.45 us -> 19 us
  between operations: 14.2 us -> 0.78 us
    reduce_scatter x2 -> x0, waiting for transfers between devices: 226 us -> none  [the longest x1 159 us: local(): lax.psum_scatter(jnp.concatenate([gate_part, up_part, back_grad], axis=1)...]
    pallas_call x0 -> x21, Pallas kernels: none -> 201 us  [chain_call(): pl.pallas_call(kernel, name=name, out_shape=out_shape, in_specs=in_specs,...]
    all_gather x5 -> x0, waiting for transfers between devices: 138 us -> none  [the longest x1 49.5 us: local(): lax.all_gather(inputs, 'row', axis=0, tiled=True)]
    dot_general x9 -> x0, matrix products: 121 us -> none  [the longest x1 15.5 us: local(): gate_part = jnp.dot(full_inputs, w_gate, preferred_element_type=jnp.float32)]
    unnamed x12 -> x0, local copies, waits for them, and re-layouts: 37.6 us -> none
    ppermute x0 -> x34, starting transfers between devices: none -> 19 us  [the longest x6 8.21 us: local(): lax.ppermute(v, 'row', [(i, (i + 1) % rows) for i in range(rows)])]
    ppermute x0 -> x34, waiting for transfers between devices: none -> 15.7 us  [the longest x24 8.71 us: local(): lax.ppermute(v, 'col', [(i, i ^ 1) for i in range(cols)])]
    concatenate x2 -> x0, other arithmetic: 14.2 us -> none  [the longest x1 10.4 us: local(): jnp.concatenate([gate_part, up_part, back_grad], axis=1)]
  transfers between devices with their start and end apart: 7 -> 34, of which waited for: 7 -> 13; matrix products, arithmetic and copies ran while one was open for 24% -> 0% of each run, Pallas kernels for 0% -> 82%
where the time goes in v1:
time: 239 us; the launch traced here: 238 us
  Pallas kernels  201 us (84%)
  starting transfers between devices  19 us (8%)
  waiting for transfers between devices  15.7 us (7%)
    pallas_call x21, Pallas kernels, chain_call(): pl.pallas_call(kernel, name=name, out_shape=out_shape, in_specs=in_specs,...  201 us
    ppermute x24, waiting for transfers between devices, local(): lax.ppermute(v, 'col', [(i, i ^ 1) for i in range(cols)])  8.71 us
    ppermute x6, starting transfers between devices, local(): lax.ppermute(v, 'row', [(i, (i + 1) % rows) for i in range(rows)])  8.21 us
    ppermute x6, waiting for transfers between devices, local(): lax.ppermute(v, 'row', [(i, (i + 1) % rows) for i in range(rows)])  6.44 us
    ppermute x24, starting transfers between devices, local(): lax.ppermute(v, 'col', [(i, i ^ 1) for i in range(cols)])  5.74 us
    ppermute x4, starting transfers between devices, local(): lax.ppermute(v, 'col', [(i, i ^ 2) for i in range(cols)])  5.01 us
  transfers between devices with their start and end apart: 34, of which 13 were waited for; matrix products, arithmetic and copies ran while one was open for 0% of the time, Pallas kernels for 82%

profile of v1, /device:TPU:0, one launch (start us, length us, event | category | flops | bytes accessed | tf_op | source)
XLA Modules:
  0.0 238.4 jit_solution(11648486876157723711)
XLA Ops:
  0.6 2.3 pad_maximum_fusion
  2.9 3.0 %collective-permute-start.4 = (bf16[2,128,2048]{2,1,0:T(8,128)(2,1)}, bf16[2,128,2048]{2,1,0:T(8,128)(2,1)}, u32[]{:S(2)}, u32[]{:S(2)}) collective-permute-start(bf16[2,128,2048]{2,1,0:T(8,128)(2,1)} %pad_maximum_fusion), channel_id=1, source_target_pairs={{0,4},{4,8},{8,12},{12,0},{1,5},{5,9},{9,13},{13,1},{2,6},{6,10},{... | collective-permute-start | bytes 3145736 | tf_op jit(solution)/shard_map/ppermute | solution.py:379
  5.9 18.0 %sums.4 = (bf16[128,1792]{1,0:T(8,128)(2,1)}, bf16[128,1792]{1,0:T(8,128)(2,1)}, bf16[128,1792]{1,0:T(8,128)(2,1)}, f32[3,128,1792]{2,1,0:T(8,128)}) custom-call(s32[1]{0:T(128)} %bitcast.s.refs_0_, bf16[128,2048]{1,0:T(8,128)(2,1)} %refs_1_.9, bf16[128,2048]{1,0:T(8,128)(2,1)} %refs_2_.15, bf16[2048,3584]{1,0:T(8,128)(2,1)} %refs_1_.8, ...), custom_call_target="tpu_custom_call" | custom-call | flops 1 | bytes 1 | tf_op jit(solution)/shard_map/sums/pallas_call | solution.py:58
  24.0 0.5 collective-permute-start.1
  24.6 1.6 collective-permute-done.refs_1_
  26.2 0.7 collective-permute-done.1.refs_2_
  26.8 0.7 collective-permute-done.2.refs_3_
  27.5 3.2 %share.4.refs_1_ = bf16[3,128,1792]{2,1,0:T(8,128)(2,1)} custom-call(f32[3,128,1792]{2,1,0:T(8,128)} %get-tuple-element.40.refs_0_, bf16[128,1792]{1,0:T(8,128)(2,1)} %collective-permute-done.refs_1_, bf16[128,1792]{1,0:T(8,128)(2,1)} %collective-permute-done.1.refs_2_, bf16[128,1792]{1,0:T(8,128)(2,1)} %collective-permute-done.2.refs_3_, ...), custom_call_target="tpu_custom_call" | custom-call | flops 1 | bytes 1 | tf_op jit(solution)/shard_map/share/pallas_call | solution.py:58
  30.6 0.8 collective-permute-done.4.refs_0_
  31.4 0.9 collective-permute-start.5
  32.3 1.5 collective-permute-start.3
  33.8 18.0 %sums.5 = (bf16[128,1792]{1,0:T(8,128)(2,1)}, bf16[128,1792]{1,0:T(8,128)(2,1)}, bf16[128,1792]{1,0:T(8,128)(2,1)}, f32[3,128,1792]{2,1,0:T(8,128)}) custom-call(s32[1]{0:T(128)} %bitcast.s.refs_0_, bf16[2,128,2048]{2,1,0:T(8,128)(2,1)} %hold.2.refs_1_.refs_5_.refs_3_, bf16[2048,3584]{1,0:T(8,128)(2,1)} %refs_1_.8, bf16[2048,3584]{1,0:T(8,128)(2,1)} %refs_2_.14, ...), custom_call_target="tpu_custom_call" | custom-call | flops 1 | bytes 1 | tf_op jit(solution)/shard_map/sums/pallas_call | solution.py:58
  51.9 0.5 collective-permute-start.7
  52.4 5.6 %collective-permute-done.5.refs_0_ = bf16[2,128,2048]{2,1,0:T(8,128)(2,1)} collective-permute-done((bf16[2,128,2048]{2,1,0:T(8,128)(2,1)}, bf16[2,128,2048]{2,1,0:T(8,128)(2,1)}, u32[]{:S(2)}, u32[]{:S(2)}) %collective-permute-start.5) | collective-permute-done | bytes 1048608 | tf_op jit(solution)/shard_map/ppermute | solution.py:379
  58.0 3.2 %share.5.refs_5_ = bf16[3,128,1792]{2,1,0:T(8,128)(2,1)} custom-call(f32[3,128,1792]{2,1,0:T(8,128)} %get-tuple-element.45.refs_0_, bf16[128,1792]{1,0:T(8,128)(2,1)} %collective-permute-done.6.refs_1_, bf16[128,1792]{1,0:T(8,128)(2,1)} %collective-permute-done.7.refs_2_, bf16[128,1792]{1,0:T(8,128)(2,1)} %collective-permute-done.8.refs_3_, ...), custom_call_target="tpu_custom_call" | custom-call | flops 1 | bytes 1 | tf_op jit(solution)/shard_map/share/pallas_call | solution.py:58
  61.2 1.5 collective-permute-start.12
  62.7 18.0 %sums.6 = (bf16[128,1792]{1,0:T(8,128)(2,1)}, bf16[128,1792]{1,0:T(8,128)(2,1)}, bf16[128,1792]{1,0:T(8,128)(2,1)}, f32[3,128,1792]{2,1,0:T(8,128)}) custom-call(s32[1]{0:T(128)} %bitcast.s.refs_0_, bf16[2,128,2048]{2,1,0:T(8,128)(2,1)} %hold.3.refs_4_.refs_1_, bf16[2048,3584]{1,0:T(8,128)(2,1)} %refs_1_.8, bf16[2048,3584]{1,0:T(8,128)(2,1)} %refs_2_.14, ...), custom_call_target="tpu_custom_call" | custom-call | flops 1 | bytes 1 | tf_op jit(solution)/shard_map/sums/pallas_call | solution.py:58
  80.8 0.5 collective-permute-start.15
  81.4 3.9 %point.4 = (bf16[128,1792]{1,0:T(8,128)(2,1)}, bf16[128,1792]{1,0:T(8,128)(2,1)}, bf16[128,1792]{1,0:T(8,128)(2,1)}) custom-call(f32[3,128,1792]{2,1,0:T(8,128)} %get-tuple-element.40.refs_0_, bf16[128,1792]{1,0:T(8,128)(2,1)} %collective-permute-done.refs_1_, bf16[128,1792]{1,0:T(8,128)(2,1)} %collective-permute-done.1.refs_2_, ...), custom_call_target="tpu_custom_call" | custom-call | flops 1 | bytes 1 | tf_op jit(solution)/shard_map/point/pallas_call | solution.py:58
  85.3 0.5 collective-permute-start.10
  85.8 3.2 %share.6.refs_5_ = bf16[3,128,1792]{2,1,0:T(8,128)(2,1)} custom-call(f32[3,128,1792]{2,1,0:T(8,128)} %get-tuple-element.52.refs_0_, bf16[128,1792]{1,0:T(8,128)(2,1)} %collective-permute-done.14.refs_1_, bf16[128,1792]{1,0:T(8,128)(2,1)} %collective-permute-done.15.refs_2_, bf16[128,1792]{1,0:T(8,128)(2,1)} %collective-permute-done.16.refs_3_, ...), custom_call_target="tpu_custom_call" | custom-call | flops 1 | bytes 1 | tf_op jit(solution)/shard_map/share/pallas_call | solution.py:58
  89.0 18.0 %sums.7 = (bf16[128,1792]{1,0:T(8,128)(2,1)}, bf16[128,1792]{1,0:T(8,128)(2,1)}, bf16[128,1792]{1,0:T(8,128)(2,1)}, f32[3,128,1792]{2,1,0:T(8,128)}) custom-call(s32[1]{0:T(128)} %bitcast.s.refs_0_, bf16[2,128,2048]{2,1,0:T(8,128)(2,1)} %collective-permute-done.13.refs_1_.refs_5_, bf16[2048,3584]{1,0:T(8,128)(2,1)} %refs_1_.8, bf16[2048,3584]{1,0:T(8,128)(2,1)} %refs_2_.14, ...), custom_call_target="tpu_custom_call" | custom-call | flops 1 | bytes 1 | tf_op jit(solution)/shard_map/sums/pallas_call | solution.py:58
  107.1 0.5 collective-permute-start.20
  108.1 0.5 collective-permute-start.24
  108.6 3.9 %point.5 = (bf16[128,1792]{1,0:T(8,128)(2,1)}, bf16[128,1792]{1,0:T(8,128)(2,1)}, bf16[128,1792]{1,0:T(8,128)(2,1)}) custom-call(f32[3,128,1792]{2,1,0:T(8,128)} %get-tuple-element.45.refs_0_, bf16[128,1792]{1,0:T(8,128)(2,1)} %collective-permute-done.6.refs_1_, bf16[128,1792]{1,0:T(8,128)(2,1)} %collective-permute-done.7.refs_2_, ...), custom_call_target="tpu_custom_call" | custom-call | flops 1 | bytes 1 | tf_op jit(solution)/shard_map/point/pallas_call | solution.py:58
  113.6 3.2 %share.7.refs_16_ = bf16[3,128,1792]{2,1,0:T(8,128)(2,1)} custom-call(f32[3,128,1792]{2,1,0:T(8,128)} %get-tuple-element.59.refs_0_, bf16[128,1792]{1,0:T(8,128)(2,1)} %collective-permute-done.20.refs_1_, bf16[128,1792]{1,0:T(8,128)(2,1)} %collective-permute-done.21.refs_2_, bf16[128,1792]{1,0:T(8,128)(2,1)} %collective-permute-done.22.refs_3_, ...), custom_call_target="tpu_custom_call" | custom-call | flops 1 | bytes 1 | tf_op jit(solution)/shard_map/share/pallas_call | solution.py:58
  116.8 20.3 %back.3 = (f32[2,128,2048]{2,1,0:T(8,128)}, bf16[2,128,2048]{2,1,0:T(8,128)(2,1)}) custom-call(s32[1]{0:T(128)} %bitcast.s.refs_0_, bf16[2048,3584]{1,0:T(8,128)(2,1)} %refs_1_.8, bf16[2048,3584]{1,0:T(8,128)(2,1)} %refs_2_.14, bf16[3584,2048]{1,0:T(8,128)(2,1)} %refs_3_.13, bf16[128,1792]{1,0:T(8,128)(2,1)} %collective-permute-done.9.refs_4_.refs_6_, ...), custom_call_target="tpu_custom_call" | custom-call | flops 1 | bytes 1 | tf_op jit(solution)/shard_map/back/pallas_call | solution.py:58
  137.2 1.4 collective-permute-start.28
  138.5 1.5 collective-permute-start.23
  140.0 0.5 collective-permute-done.24.refs_4_
  140.6 3.9 %point.6 = (bf16[128,1792]{1,0:T(8,128)(2,1)}, bf16[128,1792]{1,0:T(8,128)(2,1)}, bf16[128,1792]{1,0:T(8,128)(2,1)}) custom-call(f32[3,128,1792]{2,1,0:T(8,128)} %get-tuple-element.52.refs_0_, bf16[128,1792]{1,0:T(8,128)(2,1)} %collective-permute-done.14.refs_1_, bf16[128,1792]{1,0:T(8,128)(2,1)} %collective-permute-done.15.refs_2_, ...), custom_call_target="tpu_custom_call" | custom-call | flops 1 | bytes 1 | tf_op jit(solution)/shard_map/point/pallas_call | solution.py:58
  144.5 0.5 collective-permute-start.26
  145.0 1.6 collective-permute-done.25.refs_4_.refs_18_
  146.6 0.7 collective-permute-done.26.refs_5_.refs_19_
  147.3 0.7 collective-permute-done.27.refs_6_.refs_20_
  147.9 18.8 %back.4.refs_0_.refs_2_ = f32[2,128,2048]{2,1,0:T(8,128)} custom-call(s32[1]{0:T(128)} %bitcast.s.refs_0_, bf16[2048,3584]{1,0:T(8,128)(2,1)} %refs_1_.8, bf16[2048,3584]{1,0:T(8,128)(2,1)} %refs_2_.14, bf16[3584,2048]{1,0:T(8,128)(2,1)} %refs_3_.13, bf16[128,1792]{1,0:T(8,128)(2,1)} %collective-permute-done.25.refs_4_.refs_18_, ...), custom_call_target="tpu_custom_call" | custom-call | flops 1 | bytes 1 | tf_op jit(solution)/shard_map/back/pallas_call | solution.py:58
  166.7 2.7 %join.3.refs_5_ = bf16[2,128,2048]{2,1,0:T(8,128)(2,1)} custom-call(f32[2,128,2048]{2,1,0:T(8,128)} %back.4.refs_0_.refs_2_, bf16[2,128,2048]{2,1,0:T(8,128)(2,1)} %collective-permute-done.28.refs_1_, f32[2,128,2048]{2,1,0:T(8,128)} %back.4.refs_0_.refs_2_), custom_call_target="tpu_custom_call" | custom-call | flops 1 | bytes 1 | tf_op jit(solution)/shard_map/join/pallas_call | solution.py:58
  169.4 1.7 collective-permute-start.32
  171.1 3.9 %point.7 = (bf16[128,1792]{1,0:T(8,128)(2,1)}, bf16[128,1792]{1,0:T(8,128)(2,1)}, bf16[128,1792]{1,0:T(8,128)(2,1)}) custom-call(f32[3,128,1792]{2,1,0:T(8,128)} %get-tuple-element.59.refs_0_, bf16[128,1792]{1,0:T(8,128)(2,1)} %collective-permute-done.20.refs_1_, bf16[128,1792]{1,0:T(8,128)(2,1)} %collective-permute-done.21.refs_2_, ...), custom_call_target="tpu_custom_call" | custom-call | flops 1 | bytes 1 | tf_op jit(solution)/shard_map/point/pallas_call | solution.py:58
  175.0 0.5 collective-permute-start.30
  175.6 1.6 collective-permute-done.29.refs_4_.refs_24_
  177.2 0.7 collective-permute-done.30.refs_5_.refs_25_
  177.8 0.7 collective-permute-done.31.refs_6_.refs_26_
  178.5 18.8 %back.5.refs_0_.refs_2_ = f32[2,128,2048]{2,1,0:T(8,128)} custom-call(s32[1]{0:T(128)} %bitcast.s.refs_0_, bf16[2048,3584]{1,0:T(8,128)(2,1)} %refs_1_.8, bf16[2048,3584]{1,0:T(8,128)(2,1)} %refs_2_.14, bf16[3584,2048]{1,0:T(8,128)(2,1)} %refs_3_.13, bf16[128,1792]{1,0:T(8,128)(2,1)} %collective-permute-done.29.refs_4_.refs_24_, ...), custom_call_target="tpu_custom_call" | custom-call | flops 1 | bytes 1 | tf_op jit(solution)/shard_map/back/pallas_call | solution.py:58
  197.3 2.7 %join.4.refs_30_ = bf16[2,128,2048]{2,1,0:T(8,128)(2,1)} custom-call(f32[2,128,2048]{2,1,0:T(8,128)} %back.5.refs_0_.refs_2_, bf16[2,128,2048]{2,1,0:T(8,128)(2,1)} %collective-permute-done.32.refs_1_, f32[2,128,2048]{2,1,0:T(8,128)} %back.5.refs_0_.refs_2_), custom_call_target="tpu_custom_call" | custom-call | flops 1 | bytes 1 | tf_op jit(solution)/shard_map/join/pallas_call | solution.py:58
  200.1 1.2 collective-permute-start.33
  201.3 34.3 %grads.1 = (bf16[2048,3584]{1,0:T(8,128)(2,1)}, bf16[2048,3584]{1,0:T(8,128)(2,1)}, bf16[3584,2048]{1,0:T(8,128)(2,1)}) custom-call(s32[1]{0:T(128)} %bitcast.s.refs_0_, bf16[128,2048]{1,0:T(8,128)(2,1)} %refs_1_.9, bf16[128,2048]{1,0:T(8,128)(2,1)} %refs_2_.15, bf16[2,128,2048]{2,1,0:T(8,128)(2,1)} %hold.2.refs_1_.refs_5_.refs_3_, ...), custom_call_target="tpu_custom_call" | custom-call | flops 1 | bytes 1 | tf_op jit(solution)/shard_map/grads/pallas_call | solution.py:58
  235.7 2.7 %join.5 = (bf16[128,2048]{1,0:T(8,128)(2,1)}, bf16[128,2048]{1,0:T(8,128)(2,1)}) custom-call(f32[2,128,2048]{2,1,0:T(8,128)} %get-tuple-element.62.refs_5_.refs_0_, bf16[2,128,2048]{2,1,0:T(8,128)(2,1)} %collective-permute-done.33.refs_1_, bf16[2048,3584]{1,0:T(8,128)(2,1)} %get-tuple-element.37.refs_2_), custom_call_target="tpu_custom_call" | custom-call | flops 1 | bytes 1 | tf_op jit(solution)/shard_map/join/pallas_call | solution.py:58
  (42 shorter events, 2.4 us)
Async XLA Ops:
  2.9 28.5 %collective-permute-start.4 = (bf16[2,128,2048]{2,1,0:T(8,128)(2,1)}, bf16[2,128,2048]{2,1,0:T(8,128)(2,1)}, u32[]{:S(2)}, u32[]{:S(2)}) collective-permute-start(bf16[2,128,2048]{2,1,0:T(8,128)(2,1)} %pad_maximum_fusion), channel_id=1, source_target_pairs={{0,4},{4,8},{8,12},{12,0},{1,5},{5,9},{9,13},{13,1},{2,6},{6,10},{... | collective-permute-start | bytes 3145736 | tf_op jit(solution)/shard_map/ppermute | solution.py:379
  23.9 2.2 collective-permute-start
  24.0 2.8 %collective-permute-start.1 = (bf16[128,1792]{1,0:T(8,128)(2,1)}, bf16[128,1792]{1,0:T(8,128)(2,1)}, u32[]{:S(2)}, u32[]{:S(2)}) collective-permute-start(bf16[128,1792]{1,0:T(8,128)(2,1)} %get-tuple-element.42), channel_id=1, source_target_pairs={{0,1},{1,0},{2,3},{3,2},{4,5},{5,4},{6,7},{7,6},{8,9},{9,8},{10,11... | collective-permute-start | bytes 1376264 | tf_op jit(solution)/shard_map/ppermute | solution.py:377
  24.5 3.0 %collective-permute-start.2 = (bf16[128,1792]{1,0:T(8,128)(2,1)}, bf16[128,1792]{1,0:T(8,128)(2,1)}, u32[]{:S(2)}, u32[]{:S(2)}) collective-permute-start(bf16[128,1792]{1,0:T(8,128)(2,1)} %get-tuple-element.43), channel_id=1, source_target_pairs={{0,1},{1,0},{2,3},{3,2},{4,5},{5,4},{6,7},{7,6},{8,9},{9,8},{10,11... | collective-permute-start | bytes 1376264 | tf_op jit(solution)/shard_map/ppermute | solution.py:377
  31.4 26.6 %collective-permute-start.5 = (bf16[2,128,2048]{2,1,0:T(8,128)(2,1)}, bf16[2,128,2048]{2,1,0:T(8,128)(2,1)}, u32[]{:S(2)}, u32[]{:S(2)}) collective-permute-start(bf16[2,128,2048]{2,1,0:T(8,128)(2,1)} %hold.2.refs_1_.refs_5_.refs_3_), channel_id=1, source_target_pairs={{0,4},{4,8},{8,12},{12,0},{1,5},{5,9},{9,13},{13,1},{2,6},{6,10},{... | collective-permute-start | bytes 3145736 | tf_op jit(solution)/shard_map/ppermute | solution.py:379
  32.3 49.0 %collective-permute-start.3 = (bf16[3,128,1792]{2,1,0:T(8,128)(2,1)}, bf16[3,128,1792]{2,1,0:T(8,128)(2,1)}, u32[]{:S(2)}, u32[]{:S(2)}) collective-permute-start(bf16[3,128,1792]{2,1,0:T(8,128)(2,1)} %share.4.refs_1_), channel_id=1, source_target_pairs={{0,2},{1,3},{2,0},{3,1},{4,6},{5,7},{6,4},{7,5},{8,10},{9,11},{10,... | collective-permute-start | bytes 4128776 | tf_op jit(solution)/shard_map/ppermute | solution.py:378
  51.8 6.2 %collective-permute-start.6 = (bf16[128,1792]{1,0:T(8,128)(2,1)}, bf16[128,1792]{1,0:T(8,128)(2,1)}, u32[]{:S(2)}, u32[]{:S(2)}) collective-permute-start(bf16[128,1792]{1,0:T(8,128)(2,1)} %get-tuple-element.44.refs_1_), channel_id=1, source_target_pairs={{0,1},{1,0},{2,3},{3,2},{4,5},{5,4},{6,7},{7,6},{8,9},{9,8},{10,11... | collective-permute-start | bytes 1376264 | tf_op jit(solution)/shard_map/ppermute | solution.py:377
  51.9 6.2 %collective-permute-start.7 = (bf16[128,1792]{1,0:T(8,128)(2,1)}, bf16[128,1792]{1,0:T(8,128)(2,1)}, u32[]{:S(2)}, u32[]{:S(2)}) collective-permute-start(bf16[128,1792]{1,0:T(8,128)(2,1)} %get-tuple-element.46), channel_id=1, source_target_pairs={{0,1},{1,0},{2,3},{3,2},{4,5},{5,4},{6,7},{7,6},{8,9},{9,8},{10,11... | collective-permute-start | bytes 1376264 | tf_op jit(solution)/shard_map/ppermute | solution.py:377
  52.4 5.7 %collective-permute-start.8 = (bf16[128,1792]{1,0:T(8,128)(2,1)}, bf16[128,1792]{1,0:T(8,128)(2,1)}, u32[]{:S(2)}, u32[]{:S(2)}) collective-permute-start(bf16[128,1792]{1,0:T(8,128)(2,1)} %get-tuple-element.47), channel_id=1, source_target_pairs={{0,1},{1,0},{2,3},{3,2},{4,5},{5,4},{6,7},{7,6},{8,9},{9,8},{10,11... | collective-permute-start | bytes 1376264 | tf_op jit(solution)/shard_map/ppermute | solution.py:377
  61.2 46.9 %collective-permute-start.12 = (bf16[3,128,1792]{2,1,0:T(8,128)(2,1)}, bf16[3,128,1792]{2,1,0:T(8,128)(2,1)}, u32[]{:S(2)}, u32[]{:S(2)}) collective-permute-start(bf16[3,128,1792]{2,1,0:T(8,128)(2,1)} %share.5.refs_5_), channel_id=1, source_target_pairs={{0,2},{1,3},{2,0},{3,1},{4,6},{5,7},{6,4},{7,5},{8,10},{9,11},{10,... | collective-permute-start | bytes 4128776 | tf_op jit(solution)/shard_map/ppermute | solution.py:378
  62.7 26.3 %collective-permute-start.13 = (bf16[2,128,2048]{2,1,0:T(8,128)(2,1)}, bf16[2,128,2048]{2,1,0:T(8,128)(2,1)}, u32[]{:S(2)}, u32[]{:S(2)}) collective-permute-start(bf16[2,128,2048]{2,1,0:T(8,128)(2,1)} %hold.3.refs_4_.refs_1_), channel_id=1, source_target_pairs={{0,4},{4,8},{8,12},{12,0},{1,5},{5,9},{9,13},{13,1},{2,6},{6,10},{... | collective-permute-start | bytes 3145736 | tf_op jit(solution)/shard_map/ppermute | solution.py:379
  80.7 4.5 %collective-permute-start.14 = (bf16[128,1792]{1,0:T(8,128)(2,1)}, bf16[128,1792]{1,0:T(8,128)(2,1)}, u32[]{:S(2)}, u32[]{:S(2)}) collective-permute-start(bf16[128,1792]{1,0:T(8,128)(2,1)} %get-tuple-element.48.refs_5_), channel_id=1, source_target_pairs={{0,1},{1,0},{2,3},{3,2},{4,5},{5,4},{6,7},{7,6},{8,9},{9,8},{10,11... | collective-permute-start | bytes 1376264 | tf_op jit(solution)/shard_map/ppermute | solution.py:377
  80.8 5.0 %collective-permute-start.15 = (bf16[128,1792]{1,0:T(8,128)(2,1)}, bf16[128,1792]{1,0:T(8,128)(2,1)}, u32[]{:S(2)}, u32[]{:S(2)}) collective-permute-start(bf16[128,1792]{1,0:T(8,128)(2,1)} %get-tuple-element.53), channel_id=1, source_target_pairs={{0,1},{1,0},{2,3},{3,2},{4,5},{5,4},{6,7},{7,6},{8,9},{9,8},{10,11... | collective-permute-start | bytes 1376264 | tf_op jit(solution)/shard_map/ppermute | solution.py:377
  81.3 4.6 %collective-permute-start.16 = (bf16[128,1792]{1,0:T(8,128)(2,1)}, bf16[128,1792]{1,0:T(8,128)(2,1)}, u32[]{:S(2)}, u32[]{:S(2)}) collective-permute-start(bf16[128,1792]{1,0:T(8,128)(2,1)} %get-tuple-element.54), channel_id=1, source_target_pairs={{0,1},{1,0},{2,3},{3,2},{4,5},{5,4},{6,7},{7,6},{8,9},{9,8},{10,11... | collective-permute-start | bytes 1376264 | tf_op jit(solution)/shard_map/ppermute | solution.py:377
  85.3 22.4 %collective-permute-start.10 = (bf16[128,1792]{1,0:T(8,128)(2,1)}, bf16[128,1792]{1,0:T(8,128)(2,1)}, u32[]{:S(2)}, u32[]{:S(2)}) collective-permute-start(bf16[128,1792]{1,0:T(8,128)(2,1)} %get-tuple-element.50.refs_8_.refs_10_), channel_id=1, source_target_pairs={{0,1},{1,0},{2,3},{3,2},{4,5},{5,4},{6,7},{7,6},{8,9},{9,8},{10,11... | collective-permute-start | bytes 1376264 | tf_op jit(solution)/shard_map/ppermute | solution.py:377
  85.8 26.8 %collective-permute-start.11 = (bf16[128,1792]{1,0:T(8,128)(2,1)}, bf16[128,1792]{1,0:T(8,128)(2,1)}, u32[]{:S(2)}, u32[]{:S(2)}) collective-permute-start(bf16[128,1792]{1,0:T(8,128)(2,1)} %get-tuple-element.51.refs_9_.refs_11_), channel_id=1, source_target_pairs={{0,1},{1,0},{2,3},{3,2},{4,5},{5,4},{6,7},{7,6},{8,9},{9,8},{10,11... | collective-permute-start | bytes 1376264 | tf_op jit(solution)/shard_map/ppermute | solution.py:377
  107.1 5.5 %collective-permute-start.20 = (bf16[128,1792]{1,0:T(8,128)(2,1)}, bf16[128,1792]{1,0:T(8,128)(2,1)}, u32[]{:S(2)}, u32[]{:S(2)}) collective-permute-start(bf16[128,1792]{1,0:T(8,128)(2,1)} %get-tuple-element.55.refs_5_), channel_id=1, source_target_pairs={{0,1},{1,0},{2,3},{3,2},{4,5},{5,4},{6,7},{7,6},{8,9},{9,8},{10,11... | collective-permute-start | bytes 1376264 | tf_op jit(solution)/shard_map/ppermute | solution.py:377
  107.6 5.5 %collective-permute-start.21 = (bf16[128,1792]{1,0:T(8,128)(2,1)}, bf16[128,1792]{1,0:T(8,128)(2,1)}, u32[]{:S(2)}, u32[]{:S(2)}) collective-permute-start(bf16[128,1792]{1,0:T(8,128)(2,1)} %get-tuple-element.60), channel_id=1, source_target_pairs={{0,1},{1,0},{2,3},{3,2},{4,5},{5,4},{6,7},{7,6},{8,9},{9,8},{10,11... | collective-permute-start | bytes 1376264 | tf_op jit(solution)/shard_map/ppermute | solution.py:377
  107.6 5.5 %collective-permute-start.22 = (bf16[128,1792]{1,0:T(8,128)(2,1)}, bf16[128,1792]{1,0:T(8,128)(2,1)}, u32[]{:S(2)}, u32[]{:S(2)}) collective-permute-start(bf16[128,1792]{1,0:T(8,128)(2,1)} %get-tuple-element.61), channel_id=1, source_target_pairs={{0,1},{1,0},{2,3},{3,2},{4,5},{5,4},{6,7},{7,6},{8,9},{9,8},{10,11... | collective-permute-start | bytes 1376264 | tf_op jit(solution)/shard_map/ppermute | solution.py:377
  108.1 32.5 %collective-permute-start.24 = (bf16[3,128,1792]{2,1,0:T(8,128)(2,1)}, bf16[3,128,1792]{2,1,0:T(8,128)(2,1)}, u32[]{:S(2)}, u32[]{:S(2)}) collective-permute-start(bf16[3,128,1792]{2,1,0:T(8,128)(2,1)} %share.6.refs_5_), channel_id=1, source_target_pairs={{0,2},{1,3},{2,0},{3,1},{4,6},{5,7},{6,4},{7,5},{8,10},{9,11},{10,... | collective-permute-start | bytes 4128776 | tf_op jit(solution)/shard_map/ppermute | solution.py:378
  112.5 4.3 %collective-permute-start.9 = (bf16[128,1792]{1,0:T(8,128)(2,1)}, bf16[128,1792]{1,0:T(8,128)(2,1)}, u32[]{:S(2)}, u32[]{:S(2)}) collective-permute-start(bf16[128,1792]{1,0:T(8,128)(2,1)} %get-tuple-element.49.refs_4_.refs_7_.refs_9_), channel_id=1, source_target_pairs={{0,1},{1,0},{2,3},{3,2},{4,5},{5,4},{6,7},{7,6},{8,9},{9,8},{10,11... | collective-permute-start | bytes 1376264 | tf_op jit(solution)/shard_map/ppermute | solution.py:377
  112.6 4.2 %collective-permute-start.17 = (bf16[128,1792]{1,0:T(8,128)(2,1)}, bf16[128,1792]{1,0:T(8,128)(2,1)}, u32[]{:S(2)}, u32[]{:S(2)}) collective-permute-start(bf16[128,1792]{1,0:T(8,128)(2,1)} %get-tuple-element.56.refs_4_.refs_13_.refs_15_), channel_id=1, source_target_pairs={{0,1},{1,0},{2,3},{3,2},{4,5},{5,4},{6,7},{7,6},{8,9},{9,8},{10,11... | collective-permute-start | bytes 1376264 | tf_op jit(solution)/shard_map/ppermute | solution.py:377
  113.1 3.7 %collective-permute-start.18 = (bf16[128,1792]{1,0:T(8,128)(2,1)}, bf16[128,1792]{1,0:T(8,128)(2,1)}, u32[]{:S(2)}, u32[]{:S(2)}) collective-permute-start(bf16[128,1792]{1,0:T(8,128)(2,1)} %get-tuple-element.57.refs_14_.refs_16_), channel_id=1, source_target_pairs={{0,1},{1,0},{2,3},{3,2},{4,5},{5,4},{6,7},{7,6},{8,9},{9,8},{10,11... | collective-permute-start | bytes 1376264 | tf_op jit(solution)/shard_map/ppermute | solution.py:377
  113.2 3.6 %collective-permute-start.19 = (bf16[128,1792]{1,0:T(8,128)(2,1)}, bf16[128,1792]{1,0:T(8,128)(2,1)}, u32[]{:S(2)}, u32[]{:S(2)}) collective-permute-start(bf16[128,1792]{1,0:T(8,128)(2,1)} %get-tuple-element.58.refs_15_.refs_17_), channel_id=1, source_target_pairs={{0,1},{1,0},{2,3},{3,2},{4,5},{5,4},{6,7},{7,6},{8,9},{9,8},{10,11... | collective-permute-start | bytes 1376264 | tf_op jit(solution)/shard_map/ppermute | solution.py:377
  137.2 29.5 %collective-permute-start.28 = (bf16[2,128,2048]{2,1,0:T(8,128)(2,1)}, bf16[2,128,2048]{2,1,0:T(8,128)(2,1)}, u32[]{:S(2)}, u32[]{:S(2)}) collective-permute-start(bf16[2,128,2048]{2,1,0:T(8,128)(2,1)} %get-tuple-element.66), channel_id=1, source_target_pairs={{0,4},{4,8},{8,12},{12,0},{1,5},{5,9},{9,13},{13,1},{2,6},{6,10},{... | collective-permute-start | bytes 3145736 | tf_op jit(solution)/shard_map/ppermute | solution.py:379
  138.5 32.6 %collective-permute-start.23 = (bf16[3,128,1792]{2,1,0:T(8,128)(2,1)}, bf16[3,128,1792]{2,1,0:T(8,128)(2,1)}, u32[]{:S(2)}, u32[]{:S(2)}) collective-permute-start(bf16[3,128,1792]{2,1,0:T(8,128)(2,1)} %share.7.refs_16_), channel_id=1, source_target_pairs={{0,2},{1,3},{2,0},{3,1},{4,6},{5,7},{6,4},{7,5},{8,10},{9,11},{10,... | collective-permute-start | bytes 4128776 | tf_op jit(solution)/shard_map/ppermute | solution.py:378
  144.4 2.2 collective-permute-start.25
  144.5 2.8 %collective-permute-start.26 = (bf16[128,1792]{1,0:T(8,128)(2,1)}, bf16[128,1792]{1,0:T(8,128)(2,1)}, u32[]{:S(2)}, u32[]{:S(2)}) collective-permute-start(bf16[128,1792]{1,0:T(8,128)(2,1)} %get-tuple-element.64.refs_8_.refs_22_), channel_id=1, source_target_pairs={{0,1},{1,0},{2,3},{3,2},{4,5},{5,4},{6,7},{7,6},{8,9},{9,8},{10,11... | collective-permute-start | bytes 1376264 | tf_op jit(solution)/shard_map/ppermute | solution.py:377
  145.0 3.0 %collective-permute-start.27 = (bf16[128,1792]{1,0:T(8,128)(2,1)}, bf16[128,1792]{1,0:T(8,128)(2,1)}, u32[]{:S(2)}, u32[]{:S(2)}) collective-permute-start(bf16[128,1792]{1,0:T(8,128)(2,1)} %get-tuple-element.65.refs_9_.refs_23_), channel_id=1, source_target_pairs={{0,1},{1,0},{2,3},{3,2},{4,5},{5,4},{6,7},{7,6},{8,9},{9,8},{10,11... | collective-permute-start | bytes 1376264 | tf_op jit(solution)/shard_map/ppermute | solution.py:377
  169.4 27.9 %collective-permute-start.32 = (bf16[2,128,2048]{2,1,0:T(8,128)(2,1)}, bf16[2,128,2048]{2,1,0:T(8,128)(2,1)}, u32[]{:S(2)}, u32[]{:S(2)}) collective-permute-start(bf16[2,128,2048]{2,1,0:T(8,128)(2,1)} %join.3.refs_5_), channel_id=1, source_target_pairs={{0,4},{4,8},{8,12},{12,0},{1,5},{5,9},{9,13},{13,1},{2,6},{6,10},{... | collective-permute-start | bytes 3145736 | tf_op jit(solution)/shard_map/ppermute | solution.py:379
  175.0 2.2 collective-permute-start.29
  175.0 2.8 %collective-permute-start.30 = (bf16[128,1792]{1,0:T(8,128)(2,1)}, bf16[128,1792]{1,0:T(8,128)(2,1)}, u32[]{:S(2)}, u32[]{:S(2)}) collective-permute-start(bf16[128,1792]{1,0:T(8,128)(2,1)} %get-tuple-element.68.refs_8_.refs_28_), channel_id=1, source_target_pairs={{0,1},{1,0},{2,3},{3,2},{4,5},{5,4},{6,7},{7,6},{8,9},{9,8},{10,11... | collective-permute-start | bytes 1376264 | tf_op jit(solution)/shard_map/ppermute | solution.py:377
  175.5 3.0 %collective-permute-start.31 = (bf16[128,1792]{1,0:T(8,128)(2,1)}, bf16[128,1792]{1,0:T(8,128)(2,1)}, u32[]{:S(2)}, u32[]{:S(2)}) collective-permute-start(bf16[128,1792]{1,0:T(8,128)(2,1)} %get-tuple-element.69.refs_9_.refs_29_), channel_id=1, source_target_pairs={{0,1},{1,0},{2,3},{3,2},{4,5},{5,4},{6,7},{7,6},{8,9},{9,8},{10,11... | collective-permute-start | bytes 1376264 | tf_op jit(solution)/shard_map/ppermute | solution.py:377
  200.1 35.6 %collective-permute-start.33 = (bf16[2,128,2048]{2,1,0:T(8,128)(2,1)}, bf16[2,128,2048]{2,1,0:T(8,128)(2,1)}, u32[]{:S(2)}, u32[]{:S(2)}) collective-permute-start(bf16[2,128,2048]{2,1,0:T(8,128)(2,1)} %join.4.refs_30_), channel_id=1, source_target_pairs={{0,4},{4,8},{8,12},{12,0},{1,5},{5,9},{9,13},{13,1},{2,6},{6,10},{... | collective-permute-start | bytes 3145736 | tf_op jit(solution)/shard_map/ppermute | solution.py:379

commit v2 on v1

--- a/solution.py
+++ b/solution.py
@@ -364,7 +364,7 @@
     )
 
 
-ORDER = ["S0", "A0", "W1", "S1", "W2", "A1", "S2", "P0", "A2", "S3", "P1", "A3", "B01", "P2", "B2"]
+ORDER = ["S0", "A0", "W1", "S1", "A1", "W2", "S2", "P0", "A2", "S3", "P1", "A3", "B01", "P2", "B2"]
 ORDER += ["J2", "P3", "B3", "J3", "G", "J0"]
 
 

time: 239 us -> 237 us (level)
    ppermute x6, waiting for transfers between devices: 6.44 us -> 0.72 us  [local(): lax.ppermute(v, 'row', [(i, (i + 1) % rows) for i in range(rows)])]
    ppermute x24, waiting for transfers between devices: 8.71 us -> 11.6 us  [local(): lax.ppermute(v, 'col', [(i, i ^ 1) for i in range(cols)])]
  transfers between devices with their start and end apart: 34 -> 34, of which waited for: 13 -> 15; matrix products, arithmetic and copies ran while one was open for 0% -> 0% of each run, Pallas kernels for 82% -> 83%
where the time goes in v2:
time: 237 us
  Pallas kernels  201 us (85%)
  starting transfers between devices  18.3 us (8%)
  waiting for transfers between devices  14.6 us (6%)
    pallas_call x21, Pallas kernels, chain_call(): pl.pallas_call(kernel, name=name, out_shape=out_shape, in_specs=in_specs,...  201 us
    ppermute x24, waiting for transfers between devices, local(): lax.ppermute(v, 'col', [(i, i ^ 1) for i in range(cols)])  11.6 us
    ppermute x6, starting transfers between devices, local(): lax.ppermute(v, 'row', [(i, (i + 1) % rows) for i in range(rows)])  8.51 us
    ppermute x24, starting transfers between devices, local(): lax.ppermute(v, 'col', [(i, i ^ 1) for i in range(cols)])  5.73 us
  transfers between devices with their start and end apart: 34, of which 15 were waited for; matrix products, arithmetic and copies ran while one was open for 0% of the time, Pallas kernels for 83%

profile of v2, /device:TPU:0, one launch (start us, length us, event | category | flops | bytes accessed | tf_op | source)
XLA Modules:
  0.0 236.7 jit_solution(5278963769962091719)
XLA Ops:
  0.6 2.3 pad_maximum_fusion
  2.9 3.0 %collective-permute-start.4 = (bf16[2,128,2048]{2,1,0:T(8,128)(2,1)}, bf16[2,128,2048]{2,1,0:T(8,128)(2,1)}, u32[]{:S(2)}, u32[]{:S(2)}) collective-permute-start(bf16[2,128,2048]{2,1,0:T(8,128)(2,1)} %pad_maximum_fusion), channel_id=1, source_target_pairs={{0,4},{4,8},{8,12},{12,0},{1,5},{5,9},{9,13},{13,1},{2,6},{6,10},{... | collective-permute-start | bytes 3145736 | tf_op jit(solution)/shard_map/ppermute | solution.py:379
  5.9 18.0 %sums.4 = (bf16[128,1792]{1,0:T(8,128)(2,1)}, bf16[128,1792]{1,0:T(8,128)(2,1)}, bf16[128,1792]{1,0:T(8,128)(2,1)}, f32[3,128,1792]{2,1,0:T(8,128)}) custom-call(s32[1]{0:T(128)} %bitcast.s.refs_0_, bf16[128,2048]{1,0:T(8,128)(2,1)} %refs_1_.9, bf16[128,2048]{1,0:T(8,128)(2,1)} %refs_2_.15, bf16[2048,3584]{1,0:T(8,128)(2,1)} %refs_1_.8, ...), custom_call_target="tpu_custom_call" | custom-call | flops 1 | bytes 1 | tf_op jit(solution)/shard_map/sums/pallas_call | solution.py:58
  24.0 0.5 collective-permute-start.1
  24.6 1.6 collective-permute-done.refs_1_
  26.2 0.7 collective-permute-done.1.refs_2_
  26.8 0.7 collective-permute-done.2.refs_3_
  27.5 3.2 %share.4.refs_1_ = bf16[3,128,1792]{2,1,0:T(8,128)(2,1)} custom-call(f32[3,128,1792]{2,1,0:T(8,128)} %get-tuple-element.40.refs_0_, bf16[128,1792]{1,0:T(8,128)(2,1)} %collective-permute-done.refs_1_, bf16[128,1792]{1,0:T(8,128)(2,1)} %collective-permute-done.1.refs_2_, bf16[128,1792]{1,0:T(8,128)(2,1)} %collective-permute-done.2.refs_3_, ...), custom_call_target="tpu_custom_call" | custom-call | flops 1 | bytes 1 | tf_op jit(solution)/shard_map/share/pallas_call | solution.py:58
  30.7 0.7 collective-permute-done.4.refs_0_
  31.4 0.9 collective-permute-start.5
  32.3 1.5 collective-permute-start.3
  33.8 18.0 %sums.5 = (bf16[128,1792]{1,0:T(8,128)(2,1)}, bf16[128,1792]{1,0:T(8,128)(2,1)}, bf16[128,1792]{1,0:T(8,128)(2,1)}, f32[3,128,1792]{2,1,0:T(8,128)}) custom-call(s32[1]{0:T(128)} %bitcast.s.refs_0_, bf16[2,128,2048]{2,1,0:T(8,128)(2,1)} %hold.2.refs_1_.refs_5_.refs_3_, bf16[2048,3584]{1,0:T(8,128)(2,1)} %refs_1_.8, bf16[2048,3584]{1,0:T(8,128)(2,1)} %refs_2_.14, ...), custom_call_target="tpu_custom_call" | custom-call | flops 1 | bytes 1 | tf_op jit(solution)/shard_map/sums/pallas_call | solution.py:58
  51.9 0.5 collective-permute-start.7
  52.5 1.6 collective-permute-done.6.refs_1_
  54.1 0.7 collective-permute-done.7.refs_2_
  54.7 0.7 collective-permute-done.8.refs_3_
  55.4 3.2 %share.5.refs_1_ = bf16[3,128,1792]{2,1,0:T(8,128)(2,1)} custom-call(f32[3,128,1792]{2,1,0:T(8,128)} %get-tuple-element.44.refs_0_, bf16[128,1792]{1,0:T(8,128)(2,1)} %collective-permute-done.6.refs_1_, bf16[128,1792]{1,0:T(8,128)(2,1)} %collective-permute-done.7.refs_2_, bf16[128,1792]{1,0:T(8,128)(2,1)} %collective-permute-done.8.refs_3_, ...), custom_call_target="tpu_custom_call" | custom-call | flops 1 | bytes 1 | tf_op jit(solution)/shard_map/share/pallas_call | solution.py:58
  58.6 0.5 collective-permute-start.12
  59.2 1.6 collective-permute-start.13
  60.7 18.0 %sums.6 = (bf16[128,1792]{1,0:T(8,128)(2,1)}, bf16[128,1792]{1,0:T(8,128)(2,1)}, bf16[128,1792]{1,0:T(8,128)(2,1)}, f32[3,128,1792]{2,1,0:T(8,128)}) custom-call(s32[1]{0:T(128)} %bitcast.s.refs_0_, bf16[2,128,2048]{2,1,0:T(8,128)(2,1)} %hold.3.refs_1_.refs_5_.refs_4_, bf16[2048,3584]{1,0:T(8,128)(2,1)} %refs_1_.8, bf16[2048,3584]{1,0:T(8,128)(2,1)} %refs_2_.14, ...), custom_call_target="tpu_custom_call" | custom-call | flops 1 | bytes 1 | tf_op jit(solution)/shard_map/sums/pallas_call | solution.py:58
  79.4 3.9 %point.4 = (bf16[128,1792]{1,0:T(8,128)(2,1)}, bf16[128,1792]{1,0:T(8,128)(2,1)}, bf16[128,1792]{1,0:T(8,128)(2,1)}) custom-call(f32[3,128,1792]{2,1,0:T(8,128)} %get-tuple-element.40.refs_0_, bf16[128,1792]{1,0:T(8,128)(2,1)} %collective-permute-done.refs_1_, bf16[128,1792]{1,0:T(8,128)(2,1)} %collective-permute-done.1.refs_2_, ...), custom_call_target="tpu_custom_call" | custom-call | flops 1 | bytes 1 | tf_op jit(solution)/shard_map/point/pallas_call | solution.py:58
  83.9 3.2 %share.6.refs_5_ = bf16[3,128,1792]{2,1,0:T(8,128)(2,1)} custom-call(f32[3,128,1792]{2,1,0:T(8,128)} %get-tuple-element.52.refs_0_, bf16[128,1792]{1,0:T(8,128)(2,1)} %collective-permute-done.14.refs_1_, bf16[128,1792]{1,0:T(8,128)(2,1)} %collective-permute-done.15.refs_2_, bf16[128,1792]{1,0:T(8,128)(2,1)} %collective-permute-done.16.refs_3_, ...), custom_call_target="tpu_custom_call" | custom-call | flops 1 | bytes 1 | tf_op jit(solution)/shard_map/share/pallas_call | solution.py:58
  87.1 18.0 %sums.7 = (bf16[128,1792]{1,0:T(8,128)(2,1)}, bf16[128,1792]{1,0:T(8,128)(2,1)}, bf16[128,1792]{1,0:T(8,128)(2,1)}, f32[3,128,1792]{2,1,0:T(8,128)}) custom-call(s32[1]{0:T(128)} %bitcast.s.refs_0_, bf16[2,128,2048]{2,1,0:T(8,128)(2,1)} %collective-permute-done.13.refs_1_.refs_5_, bf16[2048,3584]{1,0:T(8,128)(2,1)} %refs_1_.8, bf16[2048,3584]{1,0:T(8,128)(2,1)} %refs_2_.14, ...), custom_call_target="tpu_custom_call" | custom-call | flops 1 | bytes 1 | tf_op jit(solution)/shard_map/sums/pallas_call | solution.py:58
  106.2 1.5 collective-permute-start.24
  107.7 3.9 %point.5 = (bf16[128,1792]{1,0:T(8,128)(2,1)}, bf16[128,1792]{1,0:T(8,128)(2,1)}, bf16[128,1792]{1,0:T(8,128)(2,1)}) custom-call(f32[3,128,1792]{2,1,0:T(8,128)} %get-tuple-element.44.refs_0_, bf16[128,1792]{1,0:T(8,128)(2,1)} %collective-permute-done.6.refs_1_, bf16[128,1792]{1,0:T(8,128)(2,1)} %collective-permute-done.7.refs_2_, ...), custom_call_target="tpu_custom_call" | custom-call | flops 1 | bytes 1 | tf_op jit(solution)/shard_map/point/pallas_call | solution.py:58
  112.6 3.2 %share.7.refs_16_ = bf16[3,128,1792]{2,1,0:T(8,128)(2,1)} custom-call(f32[3,128,1792]{2,1,0:T(8,128)} %get-tuple-element.59.refs_0_, bf16[128,1792]{1,0:T(8,128)(2,1)} %collective-permute-done.20.refs_1_, bf16[128,1792]{1,0:T(8,128)(2,1)} %collective-permute-done.21.refs_2_, bf16[128,1792]{1,0:T(8,128)(2,1)} %collective-permute-done.22.refs_3_, ...), custom_call_target="tpu_custom_call" | custom-call | flops 1 | bytes 1 | tf_op jit(solution)/shard_map/share/pallas_call | solution.py:58
  115.8 20.4 %back.3 = (f32[2,128,2048]{2,1,0:T(8,128)}, bf16[2,128,2048]{2,1,0:T(8,128)(2,1)}) custom-call(s32[1]{0:T(128)} %bitcast.s.refs_0_, bf16[2048,3584]{1,0:T(8,128)(2,1)} %refs_1_.8, bf16[2048,3584]{1,0:T(8,128)(2,1)} %refs_2_.14, bf16[3584,2048]{1,0:T(8,128)(2,1)} %refs_3_.13, bf16[128,1792]{1,0:T(8,128)(2,1)} %collective-permute-done.9.refs_4_.refs_6_, ...), custom_call_target="tpu_custom_call" | custom-call | flops 1 | bytes 1 | tf_op jit(solution)/shard_map/back/pallas_call | solution.py:58
  136.5 0.5 collective-permute-start.23
  137.1 1.6 collective-permute-done.24.refs_4_
  138.7 3.9 %point.6 = (bf16[128,1792]{1,0:T(8,128)(2,1)}, bf16[128,1792]{1,0:T(8,128)(2,1)}, bf16[128,1792]{1,0:T(8,128)(2,1)}) custom-call(f32[3,128,1792]{2,1,0:T(8,128)} %get-tuple-element.52.refs_0_, bf16[128,1792]{1,0:T(8,128)(2,1)} %collective-permute-done.14.refs_1_, bf16[128,1792]{1,0:T(8,128)(2,1)} %collective-permute-done.15.refs_2_, ...), custom_call_target="tpu_custom_call" | custom-call | flops 1 | bytes 1 | tf_op jit(solution)/shard_map/point/pallas_call | solution.py:58
  142.5 0.5 collective-permute-start.26
  143.1 1.6 collective-permute-done.25.refs_4_.refs_18_
  144.7 0.7 collective-permute-done.26.refs_5_.refs_19_
  145.3 0.7 collective-permute-done.27.refs_6_.refs_20_
  146.0 18.8 %back.4.refs_0_.refs_2_ = f32[2,128,2048]{2,1,0:T(8,128)} custom-call(s32[1]{0:T(128)} %bitcast.s.refs_0_, bf16[2048,3584]{1,0:T(8,128)(2,1)} %refs_1_.8, bf16[2048,3584]{1,0:T(8,128)(2,1)} %refs_2_.14, bf16[3584,2048]{1,0:T(8,128)(2,1)} %refs_3_.13, bf16[128,1792]{1,0:T(8,128)(2,1)} %collective-permute-done.25.refs_4_.refs_18_, ...), custom_call_target="tpu_custom_call" | custom-call | flops 1 | bytes 1 | tf_op jit(solution)/shard_map/back/pallas_call | solution.py:58
  164.8 2.7 %join.3.refs_5_ = bf16[2,128,2048]{2,1,0:T(8,128)(2,1)} custom-call(f32[2,128,2048]{2,1,0:T(8,128)} %back.4.refs_0_.refs_2_, bf16[2,128,2048]{2,1,0:T(8,128)(2,1)} %collective-permute-done.28.refs_1_, f32[2,128,2048]{2,1,0:T(8,128)} %back.4.refs_0_.refs_2_), custom_call_target="tpu_custom_call" | custom-call | flops 1 | bytes 1 | tf_op jit(solution)/shard_map/join/pallas_call | solution.py:58
  167.5 0.5 collective-permute-start.32
  168.0 0.7 collective-permute-done.23.refs_4_
  168.7 3.9 %point.7 = (bf16[128,1792]{1,0:T(8,128)(2,1)}, bf16[128,1792]{1,0:T(8,128)(2,1)}, bf16[128,1792]{1,0:T(8,128)(2,1)}) custom-call(f32[3,128,1792]{2,1,0:T(8,128)} %get-tuple-element.59.refs_0_, bf16[128,1792]{1,0:T(8,128)(2,1)} %collective-permute-done.20.refs_1_, bf16[128,1792]{1,0:T(8,128)(2,1)} %collective-permute-done.21.refs_2_, ...), custom_call_target="tpu_custom_call" | custom-call | flops 1 | bytes 1 | tf_op jit(solution)/shard_map/point/pallas_call | solution.py:58
  172.6 0.5 collective-permute-start.30
  173.2 1.6 collective-permute-done.29.refs_4_.refs_24_
  174.8 0.7 collective-permute-done.30.refs_5_.refs_25_
  175.5 0.7 collective-permute-done.31.refs_6_.refs_26_
  176.1 18.8 %back.5.refs_0_.refs_2_ = f32[2,128,2048]{2,1,0:T(8,128)} custom-call(s32[1]{0:T(128)} %bitcast.s.refs_0_, bf16[2048,3584]{1,0:T(8,128)(2,1)} %refs_1_.8, bf16[2048,3584]{1,0:T(8,128)(2,1)} %refs_2_.14, bf16[3584,2048]{1,0:T(8,128)(2,1)} %refs_3_.13, bf16[128,1792]{1,0:T(8,128)(2,1)} %collective-permute-done.29.refs_4_.refs_24_, ...), custom_call_target="tpu_custom_call" | custom-call | flops 1 | bytes 1 | tf_op jit(solution)/shard_map/back/pallas_call | solution.py:58
  194.9 2.7 %join.4.refs_30_ = bf16[2,128,2048]{2,1,0:T(8,128)(2,1)} custom-call(f32[2,128,2048]{2,1,0:T(8,128)} %back.5.refs_0_.refs_2_, bf16[2,128,2048]{2,1,0:T(8,128)(2,1)} %collective-permute-done.32.refs_1_, f32[2,128,2048]{2,1,0:T(8,128)} %back.5.refs_0_.refs_2_), custom_call_target="tpu_custom_call" | custom-call | flops 1 | bytes 1 | tf_op jit(solution)/shard_map/join/pallas_call | solution.py:58
  197.6 2.1 collective-permute-start.33
  199.7 34.3 %grads.1 = (bf16[2048,3584]{1,0:T(8,128)(2,1)}, bf16[2048,3584]{1,0:T(8,128)(2,1)}, bf16[3584,2048]{1,0:T(8,128)(2,1)}) custom-call(s32[1]{0:T(128)} %bitcast.s.refs_0_, bf16[128,2048]{1,0:T(8,128)(2,1)} %refs_1_.9, bf16[128,2048]{1,0:T(8,128)(2,1)} %refs_2_.15, bf16[2,128,2048]{2,1,0:T(8,128)(2,1)} %hold.2.refs_1_.refs_5_.refs_3_, ...), custom_call_target="tpu_custom_call" | custom-call | flops 1 | bytes 1 | tf_op jit(solution)/shard_map/grads/pallas_call | solution.py:58
  234.0 2.7 %join.5 = (bf16[128,2048]{1,0:T(8,128)(2,1)}, bf16[128,2048]{1,0:T(8,128)(2,1)}) custom-call(f32[2,128,2048]{2,1,0:T(8,128)} %get-tuple-element.62.refs_5_.refs_0_, bf16[2,128,2048]{2,1,0:T(8,128)(2,1)} %collective-permute-done.33.refs_1_, bf16[2048,3584]{1,0:T(8,128)(2,1)} %get-tuple-element.37.refs_2_), custom_call_target="tpu_custom_call" | custom-call | flops 1 | bytes 1 | tf_op jit(solution)/shard_map/join/pallas_call | solution.py:58
  (42 shorter events, 4.1 us)
Async XLA Ops:
  2.9 28.5 %collective-permute-start.4 = (bf16[2,128,2048]{2,1,0:T(8,128)(2,1)}, bf16[2,128,2048]{2,1,0:T(8,128)(2,1)}, u32[]{:S(2)}, u32[]{:S(2)}) collective-permute-start(bf16[2,128,2048]{2,1,0:T(8,128)(2,1)} %pad_maximum_fusion), channel_id=1, source_target_pairs={{0,4},{4,8},{8,12},{12,0},{1,5},{5,9},{9,13},{13,1},{2,6},{6,10},{... | collective-permute-start | bytes 3145736 | tf_op jit(solution)/shard_map/ppermute | solution.py:379
  23.9 2.2 collective-permute-start
  24.0 2.8 %collective-permute-start.1 = (bf16[128,1792]{1,0:T(8,128)(2,1)}, bf16[128,1792]{1,0:T(8,128)(2,1)}, u32[]{:S(2)}, u32[]{:S(2)}) collective-permute-start(bf16[128,1792]{1,0:T(8,128)(2,1)} %get-tuple-element.42), channel_id=1, source_target_pairs={{0,1},{1,0},{2,3},{3,2},{4,5},{5,4},{6,7},{7,6},{8,9},{9,8},{10,11... | collective-permute-start | bytes 1376264 | tf_op jit(solution)/shard_map/ppermute | solution.py:377
  24.5 3.0 %collective-permute-start.2 = (bf16[128,1792]{1,0:T(8,128)(2,1)}, bf16[128,1792]{1,0:T(8,128)(2,1)}, u32[]{:S(2)}, u32[]{:S(2)}) collective-permute-start(bf16[128,1792]{1,0:T(8,128)(2,1)} %get-tuple-element.43), channel_id=1, source_target_pairs={{0,1},{1,0},{2,3},{3,2},{4,5},{5,4},{6,7},{7,6},{8,9},{9,8},{10,11... | collective-permute-start | bytes 1376264 | tf_op jit(solution)/shard_map/ppermute | solution.py:377
  31.4 27.7 %collective-permute-start.5 = (bf16[2,128,2048]{2,1,0:T(8,128)(2,1)}, bf16[2,128,2048]{2,1,0:T(8,128)(2,1)}, u32[]{:S(2)}, u32[]{:S(2)}) collective-permute-start(bf16[2,128,2048]{2,1,0:T(8,128)(2,1)} %hold.2.refs_1_.refs_5_.refs_3_), channel_id=1, source_target_pairs={{0,4},{4,8},{8,12},{12,0},{1,5},{5,9},{9,13},{13,1},{2,6},{6,10},{... | collective-permute-start | bytes 3145736 | tf_op jit(solution)/shard_map/ppermute | solution.py:379
  32.3 47.0 %collective-permute-start.3 = (bf16[3,128,1792]{2,1,0:T(8,128)(2,1)}, bf16[3,128,1792]{2,1,0:T(8,128)(2,1)}, u32[]{:S(2)}, u32[]{:S(2)}) collective-permute-start(bf16[3,128,1792]{2,1,0:T(8,128)(2,1)} %share.4.refs_1_), channel_id=1, source_target_pairs={{0,2},{1,3},{2,0},{3,1},{4,6},{5,7},{6,4},{7,5},{8,10},{9,11},{10,... | collective-permute-start | bytes 4128776 | tf_op jit(solution)/shard_map/ppermute | solution.py:378
  51.9 2.2 collective-permute-start.6
  51.9 2.8 %collective-permute-start.7 = (bf16[128,1792]{1,0:T(8,128)(2,1)}, bf16[128,1792]{1,0:T(8,128)(2,1)}, u32[]{:S(2)}, u32[]{:S(2)}) collective-permute-start(bf16[128,1792]{1,0:T(8,128)(2,1)} %get-tuple-element.46), channel_id=1, source_target_pairs={{0,1},{1,0},{2,3},{3,2},{4,5},{5,4},{6,7},{7,6},{8,9},{9,8},{10,11... | collective-permute-start | bytes 1376264 | tf_op jit(solution)/shard_map/ppermute | solution.py:377
  52.4 3.0 %collective-permute-start.8 = (bf16[128,1792]{1,0:T(8,128)(2,1)}, bf16[128,1792]{1,0:T(8,128)(2,1)}, u32[]{:S(2)}, u32[]{:S(2)}) collective-permute-start(bf16[128,1792]{1,0:T(8,128)(2,1)} %get-tuple-element.47), channel_id=1, source_target_pairs={{0,1},{1,0},{2,3},{3,2},{4,5},{5,4},{6,7},{7,6},{8,9},{9,8},{10,11... | collective-permute-start | bytes 1376264 | tf_op jit(solution)/shard_map/ppermute | solution.py:377
  58.6 47.6 %collective-permute-start.12 = (bf16[3,128,1792]{2,1,0:T(8,128)(2,1)}, bf16[3,128,1792]{2,1,0:T(8,128)(2,1)}, u32[]{:S(2)}, u32[]{:S(2)}) collective-permute-start(bf16[3,128,1792]{2,1,0:T(8,128)(2,1)} %share.5.refs_1_), channel_id=1, source_target_pairs={{0,2},{1,3},{2,0},{3,1},{4,6},{5,7},{6,4},{7,5},{8,10},{9,11},{10,... | collective-permute-start | bytes 4128776 | tf_op jit(solution)/shard_map/ppermute | solution.py:378
  59.2 28.0 %collective-permute-start.13 = (bf16[2,128,2048]{2,1,0:T(8,128)(2,1)}, bf16[2,128,2048]{2,1,0:T(8,128)(2,1)}, u32[]{:S(2)}, u32[]{:S(2)}) collective-permute-start(bf16[2,128,2048]{2,1,0:T(8,128)(2,1)} %hold.3.refs_1_.refs_5_.refs_4_), channel_id=1, source_target_pairs={{0,4},{4,8},{8,12},{12,0},{1,5},{5,9},{9,13},{13,1},{2,6},{6,10},{... | collective-permute-start | bytes 3145736 | tf_op jit(solution)/shard_map/ppermute | solution.py:379
  78.8 4.6 %collective-permute-start.14 = (bf16[128,1792]{1,0:T(8,128)(2,1)}, bf16[128,1792]{1,0:T(8,128)(2,1)}, u32[]{:S(2)}, u32[]{:S(2)}) collective-permute-start(bf16[128,1792]{1,0:T(8,128)(2,1)} %get-tuple-element.48.refs_5_), channel_id=1, source_target_pairs={{0,1},{1,0},{2,3},{3,2},{4,5},{5,4},{6,7},{7,6},{8,9},{9,8},{10,11... | collective-permute-start | bytes 1376264 | tf_op jit(solution)/shard_map/ppermute | solution.py:377
  78.9 5.0 %collective-permute-start.15 = (bf16[128,1792]{1,0:T(8,128)(2,1)}, bf16[128,1792]{1,0:T(8,128)(2,1)}, u32[]{:S(2)}, u32[]{:S(2)}) collective-permute-start(bf16[128,1792]{1,0:T(8,128)(2,1)} %get-tuple-element.53), channel_id=1, source_target_pairs={{0,1},{1,0},{2,3},{3,2},{4,5},{5,4},{6,7},{7,6},{8,9},{9,8},{10,11... | collective-permute-start | bytes 1376264 | tf_op jit(solution)/shard_map/ppermute | solution.py:377
  79.3 4.6 %collective-permute-start.16 = (bf16[128,1792]{1,0:T(8,128)(2,1)}, bf16[128,1792]{1,0:T(8,128)(2,1)}, u32[]{:S(2)}, u32[]{:S(2)}) collective-permute-start(bf16[128,1792]{1,0:T(8,128)(2,1)} %get-tuple-element.54), channel_id=1, source_target_pairs={{0,1},{1,0},{2,3},{3,2},{4,5},{5,4},{6,7},{7,6},{8,9},{9,8},{10,11... | collective-permute-start | bytes 1376264 | tf_op jit(solution)/shard_map/ppermute | solution.py:377
  83.3 22.4 %collective-permute-start.10 = (bf16[128,1792]{1,0:T(8,128)(2,1)}, bf16[128,1792]{1,0:T(8,128)(2,1)}, u32[]{:S(2)}, u32[]{:S(2)}) collective-permute-start(bf16[128,1792]{1,0:T(8,128)(2,1)} %get-tuple-element.50.refs_8_.refs_10_), channel_id=1, source_target_pairs={{0,1},{1,0},{2,3},{3,2},{4,5},{5,4},{6,7},{7,6},{8,9},{9,8},{10,11... | collective-permute-start | bytes 1376264 | tf_op jit(solution)/shard_map/ppermute | solution.py:377
  83.8 27.7 %collective-permute-start.11 = (bf16[128,1792]{1,0:T(8,128)(2,1)}, bf16[128,1792]{1,0:T(8,128)(2,1)}, u32[]{:S(2)}, u32[]{:S(2)}) collective-permute-start(bf16[128,1792]{1,0:T(8,128)(2,1)} %get-tuple-element.51.refs_9_.refs_11_), channel_id=1, source_target_pairs={{0,1},{1,0},{2,3},{3,2},{4,5},{5,4},{6,7},{7,6},{8,9},{9,8},{10,11... | collective-permute-start | bytes 1376264 | tf_op jit(solution)/shard_map/ppermute | solution.py:377
  105.2 6.4 %collective-permute-start.20 = (bf16[128,1792]{1,0:T(8,128)(2,1)}, bf16[128,1792]{1,0:T(8,128)(2,1)}, u32[]{:S(2)}, u32[]{:S(2)}) collective-permute-start(bf16[128,1792]{1,0:T(8,128)(2,1)} %get-tuple-element.55.refs_5_), channel_id=1, source_target_pairs={{0,1},{1,0},{2,3},{3,2},{4,5},{5,4},{6,7},{7,6},{8,9},{9,8},{10,11... | collective-permute-start | bytes 1376264 | tf_op jit(solution)/shard_map/ppermute | solution.py:377
  105.7 6.5 %collective-permute-start.21 = (bf16[128,1792]{1,0:T(8,128)(2,1)}, bf16[128,1792]{1,0:T(8,128)(2,1)}, u32[]{:S(2)}, u32[]{:S(2)}) collective-permute-start(bf16[128,1792]{1,0:T(8,128)(2,1)} %get-tuple-element.60), channel_id=1, source_target_pairs={{0,1},{1,0},{2,3},{3,2},{4,5},{5,4},{6,7},{7,6},{8,9},{9,8},{10,11... | collective-permute-start | bytes 1376264 | tf_op jit(solution)/shard_map/ppermute | solution.py:377
  105.8 6.5 %collective-permute-start.22 = (bf16[128,1792]{1,0:T(8,128)(2,1)}, bf16[128,1792]{1,0:T(8,128)(2,1)}, u32[]{:S(2)}, u32[]{:S(2)}) collective-permute-start(bf16[128,1792]{1,0:T(8,128)(2,1)} %get-tuple-element.61), channel_id=1, source_target_pairs={{0,1},{1,0},{2,3},{3,2},{4,5},{5,4},{6,7},{7,6},{8,9},{9,8},{10,11... | collective-permute-start | bytes 1376264 | tf_op jit(solution)/shard_map/ppermute | solution.py:377
  106.2 32.5 %collective-permute-start.24 = (bf16[3,128,1792]{2,1,0:T(8,128)(2,1)}, bf16[3,128,1792]{2,1,0:T(8,128)(2,1)}, u32[]{:S(2)}, u32[]{:S(2)}) collective-permute-start(bf16[3,128,1792]{2,1,0:T(8,128)(2,1)} %share.6.refs_5_), channel_id=1, source_target_pairs={{0,2},{1,3},{2,0},{3,1},{4,6},{5,7},{6,4},{7,5},{8,10},{9,11},{10,... | collective-permute-start | bytes 4128776 | tf_op jit(solution)/shard_map/ppermute | solution.py:378
  111.5 4.3 %collective-permute-start.9 = (bf16[128,1792]{1,0:T(8,128)(2,1)}, bf16[128,1792]{1,0:T(8,128)(2,1)}, u32[]{:S(2)}, u32[]{:S(2)}) collective-permute-start(bf16[128,1792]{1,0:T(8,128)(2,1)} %get-tuple-element.49.refs_4_.refs_7_.refs_9_), channel_id=1, source_target_pairs={{0,1},{1,0},{2,3},{3,2},{4,5},{5,4},{6,7},{7,6},{8,9},{9,8},{10,11... | collective-permute-start | bytes 1376264 | tf_op jit(solution)/shard_map/ppermute | solution.py:377
  111.6 4.2 %collective-permute-start.17 = (bf16[128,1792]{1,0:T(8,128)(2,1)}, bf16[128,1792]{1,0:T(8,128)(2,1)}, u32[]{:S(2)}, u32[]{:S(2)}) collective-permute-start(bf16[128,1792]{1,0:T(8,128)(2,1)} %get-tuple-element.56.refs_4_.refs_13_.refs_15_), channel_id=1, source_target_pairs={{0,1},{1,0},{2,3},{3,2},{4,5},{5,4},{6,7},{7,6},{8,9},{9,8},{10,11... | collective-permute-start | bytes 1376264 | tf_op jit(solution)/shard_map/ppermute | solution.py:377
  112.1 3.7 %collective-permute-start.18 = (bf16[128,1792]{1,0:T(8,128)(2,1)}, bf16[128,1792]{1,0:T(8,128)(2,1)}, u32[]{:S(2)}, u32[]{:S(2)}) collective-permute-start(bf16[128,1792]{1,0:T(8,128)(2,1)} %get-tuple-element.57.refs_14_.refs_16_), channel_id=1, source_target_pairs={{0,1},{1,0},{2,3},{3,2},{4,5},{5,4},{6,7},{7,6},{8,9},{9,8},{10,11... | collective-permute-start | bytes 1376264 | tf_op jit(solution)/shard_map/ppermute | solution.py:377
  112.2 3.6 %collective-permute-start.19 = (bf16[128,1792]{1,0:T(8,128)(2,1)}, bf16[128,1792]{1,0:T(8,128)(2,1)}, u32[]{:S(2)}, u32[]{:S(2)}) collective-permute-start(bf16[128,1792]{1,0:T(8,128)(2,1)} %get-tuple-element.58.refs_15_.refs_17_), channel_id=1, source_target_pairs={{0,1},{1,0},{2,3},{3,2},{4,5},{5,4},{6,7},{7,6},{8,9},{9,8},{10,11... | collective-permute-start | bytes 1376264 | tf_op jit(solution)/shard_map/ppermute | solution.py:377
  136.2 28.6 %collective-permute-start.28 = (bf16[2,128,2048]{2,1,0:T(8,128)(2,1)}, bf16[2,128,2048]{2,1,0:T(8,128)(2,1)}, u32[]{:S(2)}, u32[]{:S(2)}) collective-permute-start(bf16[2,128,2048]{2,1,0:T(8,128)(2,1)} %get-tuple-element.66), channel_id=1, source_target_pairs={{0,4},{4,8},{8,12},{12,0},{1,5},{5,9},{9,13},{13,1},{2,6},{6,10},{... | collective-permute-start | bytes 3145736 | tf_op jit(solution)/shard_map/ppermute | solution.py:379
  136.5 32.2 %collective-permute-start.23 = (bf16[3,128,1792]{2,1,0:T(8,128)(2,1)}, bf16[3,128,1792]{2,1,0:T(8,128)(2,1)}, u32[]{:S(2)}, u32[]{:S(2)}) collective-permute-start(bf16[3,128,1792]{2,1,0:T(8,128)(2,1)} %share.7.refs_16_), channel_id=1, source_target_pairs={{0,2},{1,3},{2,0},{3,1},{4,6},{5,7},{6,4},{7,5},{8,10},{9,11},{10,... | collective-permute-start | bytes 4128776 | tf_op jit(solution)/shard_map/ppermute | solution.py:378
  142.5 2.2 collective-permute-start.25
  142.5 2.8 %collective-permute-start.26 = (bf16[128,1792]{1,0:T(8,128)(2,1)}, bf16[128,1792]{1,0:T(8,128)(2,1)}, u32[]{:S(2)}, u32[]{:S(2)}) collective-permute-start(bf16[128,1792]{1,0:T(8,128)(2,1)} %get-tuple-element.64.refs_8_.refs_22_), channel_id=1, source_target_pairs={{0,1},{1,0},{2,3},{3,2},{4,5},{5,4},{6,7},{7,6},{8,9},{9,8},{10,11... | collective-permute-start | bytes 1376264 | tf_op jit(solution)/shard_map/ppermute | solution.py:377
  143.0 3.0 %collective-permute-start.27 = (bf16[128,1792]{1,0:T(8,128)(2,1)}, bf16[128,1792]{1,0:T(8,128)(2,1)}, u32[]{:S(2)}, u32[]{:S(2)}) collective-permute-start(bf16[128,1792]{1,0:T(8,128)(2,1)} %get-tuple-element.65.refs_9_.refs_23_), channel_id=1, source_target_pairs={{0,1},{1,0},{2,3},{3,2},{4,5},{5,4},{6,7},{7,6},{8,9},{9,8},{10,11... | collective-permute-start | bytes 1376264 | tf_op jit(solution)/shard_map/ppermute | solution.py:377
  167.5 27.4 %collective-permute-start.32 = (bf16[2,128,2048]{2,1,0:T(8,128)(2,1)}, bf16[2,128,2048]{2,1,0:T(8,128)(2,1)}, u32[]{:S(2)}, u32[]{:S(2)}) collective-permute-start(bf16[2,128,2048]{2,1,0:T(8,128)(2,1)} %join.3.refs_5_), channel_id=1, source_target_pairs={{0,4},{4,8},{8,12},{12,0},{1,5},{5,9},{9,13},{13,1},{2,6},{6,10},{... | collective-permute-start | bytes 3145736 | tf_op jit(solution)/shard_map/ppermute | solution.py:379
  172.6 2.2 collective-permute-start.29
  172.6 2.8 %collective-permute-start.30 = (bf16[128,1792]{1,0:T(8,128)(2,1)}, bf16[128,1792]{1,0:T(8,128)(2,1)}, u32[]{:S(2)}, u32[]{:S(2)}) collective-permute-start(bf16[128,1792]{1,0:T(8,128)(2,1)} %get-tuple-element.68.refs_8_.refs_28_), channel_id=1, source_target_pairs={{0,1},{1,0},{2,3},{3,2},{4,5},{5,4},{6,7},{7,6},{8,9},{9,8},{10,11... | collective-permute-start | bytes 1376264 | tf_op jit(solution)/shard_map/ppermute | solution.py:377
  173.2 3.0 %collective-permute-start.31 = (bf16[128,1792]{1,0:T(8,128)(2,1)}, bf16[128,1792]{1,0:T(8,128)(2,1)}, u32[]{:S(2)}, u32[]{:S(2)}) collective-permute-start(bf16[128,1792]{1,0:T(8,128)(2,1)} %get-tuple-element.69.refs_9_.refs_29_), channel_id=1, source_target_pairs={{0,1},{1,0},{2,3},{3,2},{4,5},{5,4},{6,7},{7,6},{8,9},{9,8},{10,11... | collective-permute-start | bytes 1376264 | tf_op jit(solution)/shard_map/ppermute | solution.py:377
  197.6 36.4 %collective-permute-start.33 = (bf16[2,128,2048]{2,1,0:T(8,128)(2,1)}, bf16[2,128,2048]{2,1,0:T(8,128)(2,1)}, u32[]{:S(2)}, u32[]{:S(2)}) collective-permute-start(bf16[2,128,2048]{2,1,0:T(8,128)(2,1)} %join.4.refs_30_), channel_id=1, source_target_pairs={{0,4},{4,8},{8,12},{12,0},{1,5},{5,9},{9,13},{13,1},{2,6},{6,10},{... | collective-permute-start | bytes 3145736 | tf_op jit(solution)/shard_map/ppermute | solution.py:379

commit v3 on v2

--- a/solution.py
+++ b/solution.py
@@ -342,7 +342,7 @@
         pltpu.emit_pipeline(
             step,
             grid=(2 * n,),
-            in_specs=results_specs(hs, t0, n, None),
+            in_specs=results_specs(hs, t0, n, DEEP),
             out_specs=weight_specs(tile, F, None),
         )(*h_hbm, gate_hbm, up_hbm, down_hbm)
 

time: 237 us -> 237 us (level)
  no operation moved by 1% of the time
where the time goes in v3:
time: 237 us
  Pallas kernels  201 us (85%)
  starting transfers between devices  18.3 us (8%)
  waiting for transfers between devices  14.6 us (6%)
    pallas_call x21, Pallas kernels, chain_call(): pl.pallas_call(kernel, name=name, out_shape=out_shape, in_specs=in_specs,...  201 us
    ppermute x24, waiting for transfers between devices, local(): lax.ppermute(v, 'col', [(i, i ^ 1) for i in range(cols)])  11.6 us
    ppermute x6, starting transfers between devices, local(): lax.ppermute(v, 'row', [(i, (i + 1) % rows) for i in range(rows)])  8.51 us
    ppermute x24, starting transfers between devices, local(): lax.ppermute(v, 'col', [(i, i ^ 1) for i in range(cols)])  5.73 us
  transfers between devices with their start and end apart: 34, of which 15 were waited for; matrix products, arithmetic and copies ran while one was open for 0% of the time, Pallas kernels for 83%

profile of v3, /device:TPU:0, one launch (start us, length us, event | category | flops | bytes accessed | tf_op | source)
XLA Modules:
  0.0 236.8 jit_solution(12849763139737448368)
XLA Ops:
  0.6 2.3 pad_maximum_fusion
  2.9 3.0 %collective-permute-start.4 = (bf16[2,128,2048]{2,1,0:T(8,128)(2,1)}, bf16[2,128,2048]{2,1,0:T(8,128)(2,1)}, u32[]{:S(2)}, u32[]{:S(2)}) collective-permute-start(bf16[2,128,2048]{2,1,0:T(8,128)(2,1)} %pad_maximum_fusion), channel_id=1, source_target_pairs={{0,4},{4,8},{8,12},{12,0},{1,5},{5,9},{9,13},{13,1},{2,6},{6,10},{... | collective-permute-start | bytes 3145736 | tf_op jit(solution)/shard_map/ppermute | solution.py:379
  5.9 18.0 %sums.4 = (bf16[128,1792]{1,0:T(8,128)(2,1)}, bf16[128,1792]{1,0:T(8,128)(2,1)}, bf16[128,1792]{1,0:T(8,128)(2,1)}, f32[3,128,1792]{2,1,0:T(8,128)}) custom-call(s32[1]{0:T(128)} %bitcast.s.refs_0_, bf16[128,2048]{1,0:T(8,128)(2,1)} %refs_1_.9, bf16[128,2048]{1,0:T(8,128)(2,1)} %refs_2_.15, bf16[2048,3584]{1,0:T(8,128)(2,1)} %refs_1_.8, ...), custom_call_target="tpu_custom_call" | custom-call | flops 1 | bytes 1 | tf_op jit(solution)/shard_map/sums/pallas_call | solution.py:58
  24.0 0.5 collective-permute-start.1
  24.6 1.6 collective-permute-done.refs_1_
  26.2 0.7 collective-permute-done.1.refs_2_
  26.8 0.7 collective-permute-done.2.refs_3_
  27.5 3.2 %share.4.refs_1_ = bf16[3,128,1792]{2,1,0:T(8,128)(2,1)} custom-call(f32[3,128,1792]{2,1,0:T(8,128)} %get-tuple-element.40.refs_0_, bf16[128,1792]{1,0:T(8,128)(2,1)} %collective-permute-done.refs_1_, bf16[128,1792]{1,0:T(8,128)(2,1)} %collective-permute-done.1.refs_2_, bf16[128,1792]{1,0:T(8,128)(2,1)} %collective-permute-done.2.refs_3_, ...), custom_call_target="tpu_custom_call" | custom-call | flops 1 | bytes 1 | tf_op jit(solution)/shard_map/share/pallas_call | solution.py:58
  30.7 0.7 collective-permute-done.4.refs_0_
  31.4 0.9 collective-permute-start.5
  32.3 1.5 collective-permute-start.3
  33.8 18.0 %sums.5 = (bf16[128,1792]{1,0:T(8,128)(2,1)}, bf16[128,1792]{1,0:T(8,128)(2,1)}, bf16[128,1792]{1,0:T(8,128)(2,1)}, f32[3,128,1792]{2,1,0:T(8,128)}) custom-call(s32[1]{0:T(128)} %bitcast.s.refs_0_, bf16[2,128,2048]{2,1,0:T(8,128)(2,1)} %hold.2.refs_1_.refs_5_.refs_3_, bf16[2048,3584]{1,0:T(8,128)(2,1)} %refs_1_.8, bf16[2048,3584]{1,0:T(8,128)(2,1)} %refs_2_.14, ...), custom_call_target="tpu_custom_call" | custom-call | flops 1 | bytes 1 | tf_op jit(solution)/shard_map/sums/pallas_call | solution.py:58
  51.9 0.5 collective-permute-start.7
  52.5 1.6 collective-permute-done.6.refs_1_
  54.1 0.7 collective-permute-done.7.refs_2_
  54.7 0.7 collective-permute-done.8.refs_3_
  55.4 3.2 %share.5.refs_1_ = bf16[3,128,1792]{2,1,0:T(8,128)(2,1)} custom-call(f32[3,128,1792]{2,1,0:T(8,128)} %get-tuple-element.44.refs_0_, bf16[128,1792]{1,0:T(8,128)(2,1)} %collective-permute-done.6.refs_1_, bf16[128,1792]{1,0:T(8,128)(2,1)} %collective-permute-done.7.refs_2_, bf16[128,1792]{1,0:T(8,128)(2,1)} %collective-permute-done.8.refs_3_, ...), custom_call_target="tpu_custom_call" | custom-call | flops 1 | bytes 1 | tf_op jit(solution)/shard_map/share/pallas_call | solution.py:58
  58.6 0.5 collective-permute-start.12
  59.2 1.6 collective-permute-start.13
  60.7 18.0 %sums.6 = (bf16[128,1792]{1,0:T(8,128)(2,1)}, bf16[128,1792]{1,0:T(8,128)(2,1)}, bf16[128,1792]{1,0:T(8,128)(2,1)}, f32[3,128,1792]{2,1,0:T(8,128)}) custom-call(s32[1]{0:T(128)} %bitcast.s.refs_0_, bf16[2,128,2048]{2,1,0:T(8,128)(2,1)} %hold.3.refs_1_.refs_5_.refs_4_, bf16[2048,3584]{1,0:T(8,128)(2,1)} %refs_1_.8, bf16[2048,3584]{1,0:T(8,128)(2,1)} %refs_2_.14, ...), custom_call_target="tpu_custom_call" | custom-call | flops 1 | bytes 1 | tf_op jit(solution)/shard_map/sums/pallas_call | solution.py:58
  79.4 3.9 %point.4 = (bf16[128,1792]{1,0:T(8,128)(2,1)}, bf16[128,1792]{1,0:T(8,128)(2,1)}, bf16[128,1792]{1,0:T(8,128)(2,1)}) custom-call(f32[3,128,1792]{2,1,0:T(8,128)} %get-tuple-element.40.refs_0_, bf16[128,1792]{1,0:T(8,128)(2,1)} %collective-permute-done.refs_1_, bf16[128,1792]{1,0:T(8,128)(2,1)} %collective-permute-done.1.refs_2_, ...), custom_call_target="tpu_custom_call" | custom-call | flops 1 | bytes 1 | tf_op jit(solution)/shard_map/point/pallas_call | solution.py:58
  83.9 3.2 %share.6.refs_5_ = bf16[3,128,1792]{2,1,0:T(8,128)(2,1)} custom-call(f32[3,128,1792]{2,1,0:T(8,128)} %get-tuple-element.52.refs_0_, bf16[128,1792]{1,0:T(8,128)(2,1)} %collective-permute-done.14.refs_1_, bf16[128,1792]{1,0:T(8,128)(2,1)} %collective-permute-done.15.refs_2_, bf16[128,1792]{1,0:T(8,128)(2,1)} %collective-permute-done.16.refs_3_, ...), custom_call_target="tpu_custom_call" | custom-call | flops 1 | bytes 1 | tf_op jit(solution)/shard_map/share/pallas_call | solution.py:58
  87.1 18.0 %sums.7 = (bf16[128,1792]{1,0:T(8,128)(2,1)}, bf16[128,1792]{1,0:T(8,128)(2,1)}, bf16[128,1792]{1,0:T(8,128)(2,1)}, f32[3,128,1792]{2,1,0:T(8,128)}) custom-call(s32[1]{0:T(128)} %bitcast.s.refs_0_, bf16[2,128,2048]{2,1,0:T(8,128)(2,1)} %collective-permute-done.13.refs_1_.refs_5_, bf16[2048,3584]{1,0:T(8,128)(2,1)} %refs_1_.8, bf16[2048,3584]{1,0:T(8,128)(2,1)} %refs_2_.14, ...), custom_call_target="tpu_custom_call" | custom-call | flops 1 | bytes 1 | tf_op jit(solution)/shard_map/sums/pallas_call | solution.py:58
  106.2 1.5 collective-permute-start.24
  107.7 3.9 %point.5 = (bf16[128,1792]{1,0:T(8,128)(2,1)}, bf16[128,1792]{1,0:T(8,128)(2,1)}, bf16[128,1792]{1,0:T(8,128)(2,1)}) custom-call(f32[3,128,1792]{2,1,0:T(8,128)} %get-tuple-element.44.refs_0_, bf16[128,1792]{1,0:T(8,128)(2,1)} %collective-permute-done.6.refs_1_, bf16[128,1792]{1,0:T(8,128)(2,1)} %collective-permute-done.7.refs_2_, ...), custom_call_target="tpu_custom_call" | custom-call | flops 1 | bytes 1 | tf_op jit(solution)/shard_map/point/pallas_call | solution.py:58
  112.6 3.2 %share.7.refs_16_ = bf16[3,128,1792]{2,1,0:T(8,128)(2,1)} custom-call(f32[3,128,1792]{2,1,0:T(8,128)} %get-tuple-element.59.refs_0_, bf16[128,1792]{1,0:T(8,128)(2,1)} %collective-permute-done.20.refs_1_, bf16[128,1792]{1,0:T(8,128)(2,1)} %collective-permute-done.21.refs_2_, bf16[128,1792]{1,0:T(8,128)(2,1)} %collective-permute-done.22.refs_3_, ...), custom_call_target="tpu_custom_call" | custom-call | flops 1 | bytes 1 | tf_op jit(solution)/shard_map/share/pallas_call | solution.py:58
  115.8 20.4 %back.3 = (f32[2,128,2048]{2,1,0:T(8,128)}, bf16[2,128,2048]{2,1,0:T(8,128)(2,1)}) custom-call(s32[1]{0:T(128)} %bitcast.s.refs_0_, bf16[2048,3584]{1,0:T(8,128)(2,1)} %refs_1_.8, bf16[2048,3584]{1,0:T(8,128)(2,1)} %refs_2_.14, bf16[3584,2048]{1,0:T(8,128)(2,1)} %refs_3_.13, bf16[128,1792]{1,0:T(8,128)(2,1)} %collective-permute-done.9.refs_4_.refs_6_, ...), custom_call_target="tpu_custom_call" | custom-call | flops 1 | bytes 1 | tf_op jit(solution)/shard_map/back/pallas_call | solution.py:58
  136.5 0.5 collective-permute-start.23
  137.1 1.6 collective-permute-done.24.refs_4_
  138.7 3.9 %point.6 = (bf16[128,1792]{1,0:T(8,128)(2,1)}, bf16[128,1792]{1,0:T(8,128)(2,1)}, bf16[128,1792]{1,0:T(8,128)(2,1)}) custom-call(f32[3,128,1792]{2,1,0:T(8,128)} %get-tuple-element.52.refs_0_, bf16[128,1792]{1,0:T(8,128)(2,1)} %collective-permute-done.14.refs_1_, bf16[128,1792]{1,0:T(8,128)(2,1)} %collective-permute-done.15.refs_2_, ...), custom_call_target="tpu_custom_call" | custom-call | flops 1 | bytes 1 | tf_op jit(solution)/shard_map/point/pallas_call | solution.py:58
  142.5 0.5 collective-permute-start.26
  143.1 1.6 collective-permute-done.25.refs_4_.refs_18_
  144.7 0.7 collective-permute-done.26.refs_5_.refs_19_
  145.3 0.7 collective-permute-done.27.refs_6_.refs_20_
  146.0 18.8 %back.4.refs_0_.refs_2_ = f32[2,128,2048]{2,1,0:T(8,128)} custom-call(s32[1]{0:T(128)} %bitcast.s.refs_0_, bf16[2048,3584]{1,0:T(8,128)(2,1)} %refs_1_.8, bf16[2048,3584]{1,0:T(8,128)(2,1)} %refs_2_.14, bf16[3584,2048]{1,0:T(8,128)(2,1)} %refs_3_.13, bf16[128,1792]{1,0:T(8,128)(2,1)} %collective-permute-done.25.refs_4_.refs_18_, ...), custom_call_target="tpu_custom_call" | custom-call | flops 1 | bytes 1 | tf_op jit(solution)/shard_map/back/pallas_call | solution.py:58
  164.8 2.7 %join.3.refs_5_ = bf16[2,128,2048]{2,1,0:T(8,128)(2,1)} custom-call(f32[2,128,2048]{2,1,0:T(8,128)} %back.4.refs_0_.refs_2_, bf16[2,128,2048]{2,1,0:T(8,128)(2,1)} %collective-permute-done.28.refs_1_, f32[2,128,2048]{2,1,0:T(8,128)} %back.4.refs_0_.refs_2_), custom_call_target="tpu_custom_call" | custom-call | flops 1 | bytes 1 | tf_op jit(solution)/shard_map/join/pallas_call | solution.py:58
  167.5 0.5 collective-permute-start.32
  168.0 0.7 collective-permute-done.23.refs_4_
  168.7 3.9 %point.7 = (bf16[128,1792]{1,0:T(8,128)(2,1)}, bf16[128,1792]{1,0:T(8,128)(2,1)}, bf16[128,1792]{1,0:T(8,128)(2,1)}) custom-call(f32[3,128,1792]{2,1,0:T(8,128)} %get-tuple-element.59.refs_0_, bf16[128,1792]{1,0:T(8,128)(2,1)} %collective-permute-done.20.refs_1_, bf16[128,1792]{1,0:T(8,128)(2,1)} %collective-permute-done.21.refs_2_, ...), custom_call_target="tpu_custom_call" | custom-call | flops 1 | bytes 1 | tf_op jit(solution)/shard_map/point/pallas_call | solution.py:58
  172.6 0.5 collective-permute-start.30
  173.2 1.6 collective-permute-done.29.refs_4_.refs_24_
  174.8 0.7 collective-permute-done.30.refs_5_.refs_25_
  175.5 0.7 collective-permute-done.31.refs_6_.refs_26_
  176.1 18.8 %back.5.refs_0_.refs_2_ = f32[2,128,2048]{2,1,0:T(8,128)} custom-call(s32[1]{0:T(128)} %bitcast.s.refs_0_, bf16[2048,3584]{1,0:T(8,128)(2,1)} %refs_1_.8, bf16[2048,3584]{1,0:T(8,128)(2,1)} %refs_2_.14, bf16[3584,2048]{1,0:T(8,128)(2,1)} %refs_3_.13, bf16[128,1792]{1,0:T(8,128)(2,1)} %collective-permute-done.29.refs_4_.refs_24_, ...), custom_call_target="tpu_custom_call" | custom-call | flops 1 | bytes 1 | tf_op jit(solution)/shard_map/back/pallas_call | solution.py:58
  194.9 2.7 %join.4.refs_30_ = bf16[2,128,2048]{2,1,0:T(8,128)(2,1)} custom-call(f32[2,128,2048]{2,1,0:T(8,128)} %back.5.refs_0_.refs_2_, bf16[2,128,2048]{2,1,0:T(8,128)(2,1)} %collective-permute-done.32.refs_1_, f32[2,128,2048]{2,1,0:T(8,128)} %back.5.refs_0_.refs_2_), custom_call_target="tpu_custom_call" | custom-call | flops 1 | bytes 1 | tf_op jit(solution)/shard_map/join/pallas_call | solution.py:58
  197.6 2.1 collective-permute-start.33
  199.7 34.4 %grads.1 = (bf16[2048,3584]{1,0:T(8,128)(2,1)}, bf16[2048,3584]{1,0:T(8,128)(2,1)}, bf16[3584,2048]{1,0:T(8,128)(2,1)}) custom-call(s32[1]{0:T(128)} %bitcast.s.refs_0_, bf16[128,2048]{1,0:T(8,128)(2,1)} %refs_1_.9, bf16[128,2048]{1,0:T(8,128)(2,1)} %refs_2_.15, bf16[2,128,2048]{2,1,0:T(8,128)(2,1)} %hold.2.refs_1_.refs_5_.refs_3_, ...), custom_call_target="tpu_custom_call" | custom-call | flops 1 | bytes 1 | tf_op jit(solution)/shard_map/grads/pallas_call | solution.py:58
  234.1 2.7 %join.5 = (bf16[128,2048]{1,0:T(8,128)(2,1)}, bf16[128,2048]{1,0:T(8,128)(2,1)}) custom-call(f32[2,128,2048]{2,1,0:T(8,128)} %get-tuple-element.62.refs_5_.refs_0_, bf16[2,128,2048]{2,1,0:T(8,128)(2,1)} %collective-permute-done.33.refs_1_, bf16[2048,3584]{1,0:T(8,128)(2,1)} %get-tuple-element.37.refs_2_), custom_call_target="tpu_custom_call" | custom-call | flops 1 | bytes 1 | tf_op jit(solution)/shard_map/join/pallas_call | solution.py:58
  (42 shorter events, 4.1 us)
Async XLA Ops:
  2.9 28.5 %collective-permute-start.4 = (bf16[2,128,2048]{2,1,0:T(8,128)(2,1)}, bf16[2,128,2048]{2,1,0:T(8,128)(2,1)}, u32[]{:S(2)}, u32[]{:S(2)}) collective-permute-start(bf16[2,128,2048]{2,1,0:T(8,128)(2,1)} %pad_maximum_fusion), channel_id=1, source_target_pairs={{0,4},{4,8},{8,12},{12,0},{1,5},{5,9},{9,13},{13,1},{2,6},{6,10},{... | collective-permute-start | bytes 3145736 | tf_op jit(solution)/shard_map/ppermute | solution.py:379
  23.9 2.2 collective-permute-start
  24.0 2.8 %collective-permute-start.1 = (bf16[128,1792]{1,0:T(8,128)(2,1)}, bf16[128,1792]{1,0:T(8,128)(2,1)}, u32[]{:S(2)}, u32[]{:S(2)}) collective-permute-start(bf16[128,1792]{1,0:T(8,128)(2,1)} %get-tuple-element.42), channel_id=1, source_target_pairs={{0,1},{1,0},{2,3},{3,2},{4,5},{5,4},{6,7},{7,6},{8,9},{9,8},{10,11... | collective-permute-start | bytes 1376264 | tf_op jit(solution)/shard_map/ppermute | solution.py:377
  24.5 3.0 %collective-permute-start.2 = (bf16[128,1792]{1,0:T(8,128)(2,1)}, bf16[128,1792]{1,0:T(8,128)(2,1)}, u32[]{:S(2)}, u32[]{:S(2)}) collective-permute-start(bf16[128,1792]{1,0:T(8,128)(2,1)} %get-tuple-element.43), channel_id=1, source_target_pairs={{0,1},{1,0},{2,3},{3,2},{4,5},{5,4},{6,7},{7,6},{8,9},{9,8},{10,11... | collective-permute-start | bytes 1376264 | tf_op jit(solution)/shard_map/ppermute | solution.py:377
  31.4 27.7 %collective-permute-start.5 = (bf16[2,128,2048]{2,1,0:T(8,128)(2,1)}, bf16[2,128,2048]{2,1,0:T(8,128)(2,1)}, u32[]{:S(2)}, u32[]{:S(2)}) collective-permute-start(bf16[2,128,2048]{2,1,0:T(8,128)(2,1)} %hold.2.refs_1_.refs_5_.refs_3_), channel_id=1, source_target_pairs={{0,4},{4,8},{8,12},{12,0},{1,5},{5,9},{9,13},{13,1},{2,6},{6,10},{... | collective-permute-start | bytes 3145736 | tf_op jit(solution)/shard_map/ppermute | solution.py:379
  32.3 47.0 %collective-permute-start.3 = (bf16[3,128,1792]{2,1,0:T(8,128)(2,1)}, bf16[3,128,1792]{2,1,0:T(8,128)(2,1)}, u32[]{:S(2)}, u32[]{:S(2)}) collective-permute-start(bf16[3,128,1792]{2,1,0:T(8,128)(2,1)} %share.4.refs_1_), channel_id=1, source_target_pairs={{0,2},{1,3},{2,0},{3,1},{4,6},{5,7},{6,4},{7,5},{8,10},{9,11},{10,... | collective-permute-start | bytes 4128776 | tf_op jit(solution)/shard_map/ppermute | solution.py:378
  51.9 2.2 collective-permute-start.6
  51.9 2.8 %collective-permute-start.7 = (bf16[128,1792]{1,0:T(8,128)(2,1)}, bf16[128,1792]{1,0:T(8,128)(2,1)}, u32[]{:S(2)}, u32[]{:S(2)}) collective-permute-start(bf16[128,1792]{1,0:T(8,128)(2,1)} %get-tuple-element.46), channel_id=1, source_target_pairs={{0,1},{1,0},{2,3},{3,2},{4,5},{5,4},{6,7},{7,6},{8,9},{9,8},{10,11... | collective-permute-start | bytes 1376264 | tf_op jit(solution)/shard_map/ppermute | solution.py:377
  52.4 3.0 %collective-permute-start.8 = (bf16[128,1792]{1,0:T(8,128)(2,1)}, bf16[128,1792]{1,0:T(8,128)(2,1)}, u32[]{:S(2)}, u32[]{:S(2)}) collective-permute-start(bf16[128,1792]{1,0:T(8,128)(2,1)} %get-tuple-element.47), channel_id=1, source_target_pairs={{0,1},{1,0},{2,3},{3,2},{4,5},{5,4},{6,7},{7,6},{8,9},{9,8},{10,11... | collective-permute-start | bytes 1376264 | tf_op jit(solution)/shard_map/ppermute | solution.py:377
  58.6 47.6 %collective-permute-start.12 = (bf16[3,128,1792]{2,1,0:T(8,128)(2,1)}, bf16[3,128,1792]{2,1,0:T(8,128)(2,1)}, u32[]{:S(2)}, u32[]{:S(2)}) collective-permute-start(bf16[3,128,1792]{2,1,0:T(8,128)(2,1)} %share.5.refs_1_), channel_id=1, source_target_pairs={{0,2},{1,3},{2,0},{3,1},{4,6},{5,7},{6,4},{7,5},{8,10},{9,11},{10,... | collective-permute-start | bytes 4128776 | tf_op jit(solution)/shard_map/ppermute | solution.py:378
  59.2 28.0 %collective-permute-start.13 = (bf16[2,128,2048]{2,1,0:T(8,128)(2,1)}, bf16[2,128,2048]{2,1,0:T(8,128)(2,1)}, u32[]{:S(2)}, u32[]{:S(2)}) collective-permute-start(bf16[2,128,2048]{2,1,0:T(8,128)(2,1)} %hold.3.refs_1_.refs_5_.refs_4_), channel_id=1, source_target_pairs={{0,4},{4,8},{8,12},{12,0},{1,5},{5,9},{9,13},{13,1},{2,6},{6,10},{... | collective-permute-start | bytes 3145736 | tf_op jit(solution)/shard_map/ppermute | solution.py:379
  78.8 4.6 %collective-permute-start.14 = (bf16[128,1792]{1,0:T(8,128)(2,1)}, bf16[128,1792]{1,0:T(8,128)(2,1)}, u32[]{:S(2)}, u32[]{:S(2)}) collective-permute-start(bf16[128,1792]{1,0:T(8,128)(2,1)} %get-tuple-element.48.refs_5_), channel_id=1, source_target_pairs={{0,1},{1,0},{2,3},{3,2},{4,5},{5,4},{6,7},{7,6},{8,9},{9,8},{10,11... | collective-permute-start | bytes 1376264 | tf_op jit(solution)/shard_map/ppermute | solution.py:377
  78.9 5.0 %collective-permute-start.15 = (bf16[128,1792]{1,0:T(8,128)(2,1)}, bf16[128,1792]{1,0:T(8,128)(2,1)}, u32[]{:S(2)}, u32[]{:S(2)}) collective-permute-start(bf16[128,1792]{1,0:T(8,128)(2,1)} %get-tuple-element.53), channel_id=1, source_target_pairs={{0,1},{1,0},{2,3},{3,2},{4,5},{5,4},{6,7},{7,6},{8,9},{9,8},{10,11... | collective-permute-start | bytes 1376264 | tf_op jit(solution)/shard_map/ppermute | solution.py:377
  79.3 4.6 %collective-permute-start.16 = (bf16[128,1792]{1,0:T(8,128)(2,1)}, bf16[128,1792]{1,0:T(8,128)(2,1)}, u32[]{:S(2)}, u32[]{:S(2)}) collective-permute-start(bf16[128,1792]{1,0:T(8,128)(2,1)} %get-tuple-element.54), channel_id=1, source_target_pairs={{0,1},{1,0},{2,3},{3,2},{4,5},{5,4},{6,7},{7,6},{8,9},{9,8},{10,11... | collective-permute-start | bytes 1376264 | tf_op jit(solution)/shard_map/ppermute | solution.py:377
  83.3 22.4 %collective-permute-start.10 = (bf16[128,1792]{1,0:T(8,128)(2,1)}, bf16[128,1792]{1,0:T(8,128)(2,1)}, u32[]{:S(2)}, u32[]{:S(2)}) collective-permute-start(bf16[128,1792]{1,0:T(8,128)(2,1)} %get-tuple-element.50.refs_8_.refs_10_), channel_id=1, source_target_pairs={{0,1},{1,0},{2,3},{3,2},{4,5},{5,4},{6,7},{7,6},{8,9},{9,8},{10,11... | collective-permute-start | bytes 1376264 | tf_op jit(solution)/shard_map/ppermute | solution.py:377
  83.8 27.7 %collective-permute-start.11 = (bf16[128,1792]{1,0:T(8,128)(2,1)}, bf16[128,1792]{1,0:T(8,128)(2,1)}, u32[]{:S(2)}, u32[]{:S(2)}) collective-permute-start(bf16[128,1792]{1,0:T(8,128)(2,1)} %get-tuple-element.51.refs_9_.refs_11_), channel_id=1, source_target_pairs={{0,1},{1,0},{2,3},{3,2},{4,5},{5,4},{6,7},{7,6},{8,9},{9,8},{10,11... | collective-permute-start | bytes 1376264 | tf_op jit(solution)/shard_map/ppermute | solution.py:377
  105.2 6.4 %collective-permute-start.20 = (bf16[128,1792]{1,0:T(8,128)(2,1)}, bf16[128,1792]{1,0:T(8,128)(2,1)}, u32[]{:S(2)}, u32[]{:S(2)}) collective-permute-start(bf16[128,1792]{1,0:T(8,128)(2,1)} %get-tuple-element.55.refs_5_), channel_id=1, source_target_pairs={{0,1},{1,0},{2,3},{3,2},{4,5},{5,4},{6,7},{7,6},{8,9},{9,8},{10,11... | collective-permute-start | bytes 1376264 | tf_op jit(solution)/shard_map/ppermute | solution.py:377
  105.7 6.5 %collective-permute-start.21 = (bf16[128,1792]{1,0:T(8,128)(2,1)}, bf16[128,1792]{1,0:T(8,128)(2,1)}, u32[]{:S(2)}, u32[]{:S(2)}) collective-permute-start(bf16[128,1792]{1,0:T(8,128)(2,1)} %get-tuple-element.60), channel_id=1, source_target_pairs={{0,1},{1,0},{2,3},{3,2},{4,5},{5,4},{6,7},{7,6},{8,9},{9,8},{10,11... | collective-permute-start | bytes 1376264 | tf_op jit(solution)/shard_map/ppermute | solution.py:377
  105.8 6.5 %collective-permute-start.22 = (bf16[128,1792]{1,0:T(8,128)(2,1)}, bf16[128,1792]{1,0:T(8,128)(2,1)}, u32[]{:S(2)}, u32[]{:S(2)}) collective-permute-start(bf16[128,1792]{1,0:T(8,128)(2,1)} %get-tuple-element.61), channel_id=1, source_target_pairs={{0,1},{1,0},{2,3},{3,2},{4,5},{5,4},{6,7},{7,6},{8,9},{9,8},{10,11... | collective-permute-start | bytes 1376264 | tf_op jit(solution)/shard_map/ppermute | solution.py:377
  106.2 32.5 %collective-permute-start.24 = (bf16[3,128,1792]{2,1,0:T(8,128)(2,1)}, bf16[3,128,1792]{2,1,0:T(8,128)(2,1)}, u32[]{:S(2)}, u32[]{:S(2)}) collective-permute-start(bf16[3,128,1792]{2,1,0:T(8,128)(2,1)} %share.6.refs_5_), channel_id=1, source_target_pairs={{0,2},{1,3},{2,0},{3,1},{4,6},{5,7},{6,4},{7,5},{8,10},{9,11},{10,... | collective-permute-start | bytes 4128776 | tf_op jit(solution)/shard_map/ppermute | solution.py:378
  111.5 4.3 %collective-permute-start.9 = (bf16[128,1792]{1,0:T(8,128)(2,1)}, bf16[128,1792]{1,0:T(8,128)(2,1)}, u32[]{:S(2)}, u32[]{:S(2)}) collective-permute-start(bf16[128,1792]{1,0:T(8,128)(2,1)} %get-tuple-element.49.refs_4_.refs_7_.refs_9_), channel_id=1, source_target_pairs={{0,1},{1,0},{2,3},{3,2},{4,5},{5,4},{6,7},{7,6},{8,9},{9,8},{10,11... | collective-permute-start | bytes 1376264 | tf_op jit(solution)/shard_map/ppermute | solution.py:377
  111.6 4.2 %collective-permute-start.17 = (bf16[128,1792]{1,0:T(8,128)(2,1)}, bf16[128,1792]{1,0:T(8,128)(2,1)}, u32[]{:S(2)}, u32[]{:S(2)}) collective-permute-start(bf16[128,1792]{1,0:T(8,128)(2,1)} %get-tuple-element.56.refs_4_.refs_13_.refs_15_), channel_id=1, source_target_pairs={{0,1},{1,0},{2,3},{3,2},{4,5},{5,4},{6,7},{7,6},{8,9},{9,8},{10,11... | collective-permute-start | bytes 1376264 | tf_op jit(solution)/shard_map/ppermute | solution.py:377
  112.1 3.7 %collective-permute-start.18 = (bf16[128,1792]{1,0:T(8,128)(2,1)}, bf16[128,1792]{1,0:T(8,128)(2,1)}, u32[]{:S(2)}, u32[]{:S(2)}) collective-permute-start(bf16[128,1792]{1,0:T(8,128)(2,1)} %get-tuple-element.57.refs_14_.refs_16_), channel_id=1, source_target_pairs={{0,1},{1,0},{2,3},{3,2},{4,5},{5,4},{6,7},{7,6},{8,9},{9,8},{10,11... | collective-permute-start | bytes 1376264 | tf_op jit(solution)/shard_map/ppermute | solution.py:377
  112.2 3.6 %collective-permute-start.19 = (bf16[128,1792]{1,0:T(8,128)(2,1)}, bf16[128,1792]{1,0:T(8,128)(2,1)}, u32[]{:S(2)}, u32[]{:S(2)}) collective-permute-start(bf16[128,1792]{1,0:T(8,128)(2,1)} %get-tuple-element.58.refs_15_.refs_17_), channel_id=1, source_target_pairs={{0,1},{1,0},{2,3},{3,2},{4,5},{5,4},{6,7},{7,6},{8,9},{9,8},{10,11... | collective-permute-start | bytes 1376264 | tf_op jit(solution)/shard_map/ppermute | solution.py:377
  136.2 28.6 %collective-permute-start.28 = (bf16[2,128,2048]{2,1,0:T(8,128)(2,1)}, bf16[2,128,2048]{2,1,0:T(8,128)(2,1)}, u32[]{:S(2)}, u32[]{:S(2)}) collective-permute-start(bf16[2,128,2048]{2,1,0:T(8,128)(2,1)} %get-tuple-element.66), channel_id=1, source_target_pairs={{0,4},{4,8},{8,12},{12,0},{1,5},{5,9},{9,13},{13,1},{2,6},{6,10},{... | collective-permute-start | bytes 3145736 | tf_op jit(solution)/shard_map/ppermute | solution.py:379
  136.5 32.2 %collective-permute-start.23 = (bf16[3,128,1792]{2,1,0:T(8,128)(2,1)}, bf16[3,128,1792]{2,1,0:T(8,128)(2,1)}, u32[]{:S(2)}, u32[]{:S(2)}) collective-permute-start(bf16[3,128,1792]{2,1,0:T(8,128)(2,1)} %share.7.refs_16_), channel_id=1, source_target_pairs={{0,2},{1,3},{2,0},{3,1},{4,6},{5,7},{6,4},{7,5},{8,10},{9,11},{10,... | collective-permute-start | bytes 4128776 | tf_op jit(solution)/shard_map/ppermute | solution.py:378
  142.5 2.2 collective-permute-start.25
  142.5 2.8 %collective-permute-start.26 = (bf16[128,1792]{1,0:T(8,128)(2,1)}, bf16[128,1792]{1,0:T(8,128)(2,1)}, u32[]{:S(2)}, u32[]{:S(2)}) collective-permute-start(bf16[128,1792]{1,0:T(8,128)(2,1)} %get-tuple-element.64.refs_8_.refs_22_), channel_id=1, source_target_pairs={{0,1},{1,0},{2,3},{3,2},{4,5},{5,4},{6,7},{7,6},{8,9},{9,8},{10,11... | collective-permute-start | bytes 1376264 | tf_op jit(solution)/shard_map/ppermute | solution.py:377
  143.0 3.0 %collective-permute-start.27 = (bf16[128,1792]{1,0:T(8,128)(2,1)}, bf16[128,1792]{1,0:T(8,128)(2,1)}, u32[]{:S(2)}, u32[]{:S(2)}) collective-permute-start(bf16[128,1792]{1,0:T(8,128)(2,1)} %get-tuple-element.65.refs_9_.refs_23_), channel_id=1, source_target_pairs={{0,1},{1,0},{2,3},{3,2},{4,5},{5,4},{6,7},{7,6},{8,9},{9,8},{10,11... | collective-permute-start | bytes 1376264 | tf_op jit(solution)/shard_map/ppermute | solution.py:377
  167.5 27.4 %collective-permute-start.32 = (bf16[2,128,2048]{2,1,0:T(8,128)(2,1)}, bf16[2,128,2048]{2,1,0:T(8,128)(2,1)}, u32[]{:S(2)}, u32[]{:S(2)}) collective-permute-start(bf16[2,128,2048]{2,1,0:T(8,128)(2,1)} %join.3.refs_5_), channel_id=1, source_target_pairs={{0,4},{4,8},{8,12},{12,0},{1,5},{5,9},{9,13},{13,1},{2,6},{6,10},{... | collective-permute-start | bytes 3145736 | tf_op jit(solution)/shard_map/ppermute | solution.py:379
  172.6 2.2 collective-permute-start.29
  172.6 2.8 %collective-permute-start.30 = (bf16[128,1792]{1,0:T(8,128)(2,1)}, bf16[128,1792]{1,0:T(8,128)(2,1)}, u32[]{:S(2)}, u32[]{:S(2)}) collective-permute-start(bf16[128,1792]{1,0:T(8,128)(2,1)} %get-tuple-element.68.refs_8_.refs_28_), channel_id=1, source_target_pairs={{0,1},{1,0},{2,3},{3,2},{4,5},{5,4},{6,7},{7,6},{8,9},{9,8},{10,11... | collective-permute-start | bytes 1376264 | tf_op jit(solution)/shard_map/ppermute | solution.py:377
  173.2 3.0 %collective-permute-start.31 = (bf16[128,1792]{1,0:T(8,128)(2,1)}, bf16[128,1792]{1,0:T(8,128)(2,1)}, u32[]{:S(2)}, u32[]{:S(2)}) collective-permute-start(bf16[128,1792]{1,0:T(8,128)(2,1)} %get-tuple-element.69.refs_9_.refs_29_), channel_id=1, source_target_pairs={{0,1},{1,0},{2,3},{3,2},{4,5},{5,4},{6,7},{7,6},{8,9},{9,8},{10,11... | collective-permute-start | bytes 1376264 | tf_op jit(solution)/shard_map/ppermute | solution.py:377
  197.6 36.5 %collective-permute-start.33 = (bf16[2,128,2048]{2,1,0:T(8,128)(2,1)}, bf16[2,128,2048]{2,1,0:T(8,128)(2,1)}, u32[]{:S(2)}, u32[]{:S(2)}) collective-permute-start(bf16[2,128,2048]{2,1,0:T(8,128)(2,1)} %join.4.refs_30_), channel_id=1, source_target_pairs={{0,4},{4,8},{8,12},{12,0},{1,5},{5,9},{9,13},{13,1},{2,6},{6,10},{... | collective-permute-start | bytes 3145736 | tf_op jit(solution)/shard_map/ppermute | solution.py:379
